TPU v7x, 32 devices: a whole 2x2x4 slice. The times are simulated.
32 devices in a mesh: dp: 8 (over z, y), tensor: 4 (over x, core).
Axes of the slice: x: 2, y: 2, z: 4, core: 2. Of those that a mesh axis runs over, the one named last changes fastest.
Arguments:
- tokens: bfloat16 [4096, 16384], P('dp', 'tensor'), may hold values from -6 to 6
- queries: bfloat16 [4096, 4096], P('dp', 'tensor'), as said below
- out_grad: bfloat16 [4096, 4096], P('dp', 'tensor'), may hold values from -6 to 6
- key_weight: bfloat16 [16384, 256], P('tensor'), may hold values from -0.0625 to 0.0625
- value_weight: bfloat16 [16384, 256], P('tensor'), may hold values from -0.0625 to 0.0625
- key_scale: float32 [32, 256], replicated, may hold values from 0.1 to 1.9
- value_scale: float32 [32, 256], replicated, may hold values from 0.1 to 1.9
- segment_ids: int32 [8, 512], P('dp'), may hold values from 0 to 3, never falling along the last dimension, each value on 1 to 256 neighbouring positions
- tenant_ids: int32 [8, 4], P('dp'), may hold values from 0 to 31
Outputs:
- input_grad: bfloat16 [4096, 16384], P('dp', 'tensor')
- key_scale_grad: float32 [32, 256], P(None, 'tensor')
- value_scale_grad: float32 [32, 256], P(None, 'tensor')
Inputs may be any that keep to these rules, and one draw needn't show every extreme that they name: `segment_ids`: in each token group the sequence number never falls, all 4 sequences are present, and the longest holds exactly 256 tokens. `queries`: entries lie between -160 and 160.
All inputs are finite; a program needn't handle non-finite values.
Results may differ from a plain program's by a relative error of at most 0.034.
The roundings to bfloat16 on the way count: a program that leaves them out, or rounds other values in their place, can miss the bound.
Values may be sent and summed in bfloat16 or wider, within the bound.
A program may use at most 128 MiB of HBM per device.

v0:
```python
import jax
import jax.numpy as jnp
from jax import lax
from jax.sharding import PartitionSpec as P

SEQS = 4
NT = 32


def swapped(array, axis, bit):
    return lax.ppermute(array, axis, [(i, i ^ 1 << bit) for i in range(lax.axis_size(axis))])


def tenant_rows(segments, tenants):
    seq_match = segments[:, None] == jnp.arange(SEQS, dtype=jnp.int32)[None, :]
    tenant_tok = jnp.sum(jnp.where(seq_match, tenants[None, :], 0), axis=1)
    return (tenant_tok[:, None] == jnp.arange(NT, dtype=jnp.int32)[None, :]).astype(jnp.float32)


def allowed_mask(segments):
    position = jnp.arange(segments.shape[0], dtype=jnp.int32)
    return (segments[:, None] == segments[None, :]) & (position[None, :] <= position[:, None])


def head_grads(query_head, out_head, key_tile, value_tile, allowed):
    score_scale = key_tile.shape[1] ** (-0.5)
    scores = (
        lax.dot_general(
            query_head, key_tile, (((1,), (1,)), ((), ())), preferred_element_type=jnp.float32
        )
        * score_scale
    )
    scores = jnp.where(allowed, scores, -1e30)
    row_peak = jnp.max(scores, axis=1, keepdims=True)
    exp_scores = jnp.exp(scores - row_peak)
    probs = exp_scores / jnp.sum(exp_scores, axis=1, keepdims=True)
    probs_low = probs.astype(jnp.bfloat16)
    attended = jnp.dot(probs_low, value_tile, preferred_element_type=jnp.float32)
    row_delta = jnp.sum(out_head.astype(jnp.float32) * attended, axis=1, keepdims=True)
    prob_grad = lax.dot_general(
        out_head, value_tile, (((1,), (1,)), ((), ())), preferred_element_type=jnp.float32
    )
    score_grad = (probs * (prob_grad - row_delta)).astype(jnp.bfloat16)
    value_grad = lax.dot_general(
        probs_low, out_head, (((0,), (0,)), ((), ())), preferred_element_type=jnp.float32
    )
    key_grad = (
        lax.dot_general(
            score_grad, query_head, (((0,), (0,)), ((), ())), preferred_element_type=jnp.float32
        )
        * score_scale
    )
    return (key_grad, value_grad)


def contract_rows(left, weight):
    return lax.dot_general(
        left, weight, (((1,), (1,)), ((), ())), preferred_element_type=jnp.float32
    )


def on_device(
    tokens,
    queries,
    out_grad,
    key_weight,
    value_weight,
    key_scale,
    value_scale,
    segment_ids,
    tenant_ids,
):
    tensor_size = lax.axis_size("tensor")
    tensor_rank = lax.axis_index("tensor")
    member_bit = tensor_rank % 2
    head_width = key_scale.shape[1] * 2 // tensor_size
    half_width = head_width // 2
    token_count = tokens.shape[0]
    heads_here = queries.shape[1] // head_width
    tenant_hot = tenant_rows(segment_ids[0], tenant_ids[0])
    key_factor = jnp.dot(tenant_hot, key_scale, precision=lax.Precision.HIGHEST)
    value_factor = jnp.dot(tenant_hot, value_scale, precision=lax.Precision.HIGHEST)
    own_start = tensor_rank * half_width
    key_own_factor = lax.dynamic_slice_in_dim(key_factor, own_start, half_width, 1)
    value_own_factor = lax.dynamic_slice_in_dim(value_factor, own_start, half_width, 1)
    key_partial_sum = jnp.dot(tokens, key_weight, preferred_element_type=jnp.float32)
    value_partial_sum = jnp.dot(tokens, value_weight, preferred_element_type=jnp.float32)
    key_base, value_base = (
        lax.psum_scatter(key_partial_sum, "tensor", scatter_dimension=1, tiled=True),
        lax.psum_scatter(value_partial_sum, "tensor", scatter_dimension=1, tiled=True),
    )
    key_mine = (key_base * key_own_factor).astype(jnp.bfloat16)
    value_mine = (value_base * value_own_factor).astype(jnp.bfloat16)
    key_partner, value_partner = swapped((key_mine, value_mine), "tensor", 0)
    key_tile = jnp.where(
        member_bit == 0,
        jnp.concatenate([key_mine, key_partner], 1),
        jnp.concatenate([key_partner, key_mine], 1),
    )
    value_tile = jnp.where(
        member_bit == 0,
        jnp.concatenate([value_mine, value_partner], 1),
        jnp.concatenate([value_partner, value_mine], 1),
    )
    allowed = allowed_mask(segment_ids[0])

    def one_head(head_index, totals):
        column = head_index * head_width
        query_head = lax.dynamic_slice_in_dim(queries, column, head_width, 1)
        out_head = lax.dynamic_slice_in_dim(out_grad, column, head_width, 1)
        key_part, value_part = head_grads(query_head, out_head, key_tile, value_tile, allowed)
        return (totals[0] + key_part, totals[1] + value_part)

    zeros_tile = jnp.zeros((token_count, head_width), jnp.float32)
    key_partial, value_partial = lax.fori_loop(0, heads_here, one_head, (zeros_tile, zeros_tile))
    partials = jnp.concatenate([key_partial, value_partial], axis=1)
    gathered = lax.all_gather(partials.astype(jnp.bfloat16), "tensor", axis=1, tiled=True).astype(
        partials.dtype
    )
    shaped = gathered.reshape(token_count, tensor_size // 2, 2, 2, head_width)
    summed = jnp.sum(shaped, axis=2)
    key_grad = summed[:, :, 0, :].reshape(token_count, key_scale.shape[1])
    value_grad = summed[:, :, 1, :].reshape(token_count, key_scale.shape[1])
    key_low = (key_grad * key_factor).astype(jnp.bfloat16)
    value_low = (value_grad * value_factor).astype(jnp.bfloat16)
    input_grad = contract_rows(key_low, key_weight) + contract_rows(value_low, value_weight)
    key_grad_own = lax.dynamic_slice_in_dim(key_grad, own_start, half_width, 1)
    value_grad_own = lax.dynamic_slice_in_dim(value_grad, own_start, half_width, 1)
    key_tenant = lax.dot_general(
        tenant_hot,
        key_grad_own * key_base,
        (((0,), (0,)), ((), ())),
        precision=lax.Precision.HIGHEST,
    )
    value_tenant = lax.dot_general(
        tenant_hot,
        value_grad_own * value_base,
        (((0,), (0,)), ((), ())),
        precision=lax.Precision.HIGHEST,
    )
    key_total, value_total = lax.psum((key_tenant, value_tenant), "dp")
    return (input_grad.astype(jnp.bfloat16), key_total, value_total)


def solution(mesh):
    return jax.shard_map(
        on_device,
        mesh=mesh,
        in_specs=(
            P("dp", "tensor"),
            P("dp", "tensor"),
            P("dp", "tensor"),
            P("tensor", None),
            P("tensor", None),
            P(),
            P(),
            P("dp", None),
            P("dp", None),
        ),
        out_specs=(P("dp", "tensor"), P(None, "tensor"), P(None, "tensor")),
        check_vma=False,
    )
```

profile of v0, /device:TPU:0, one launch (start us, length us, event | category | flops | bytes accessed | tf_op | source)
XLA Modules:
  0.0 219.5 jit_solution(2867920145792026931)
XLA Ops:
  7.2 5.1 %fusion.40 = f32[512,256]{0,1:T(8,128)} fusion(bf16[512,4096]{1,0:T(8,128)(2,1)} %param.11, bf16[4096,256]{1,0:T(8,128)(2,1)} %param.15), kind=kOutput, calls=%fused_computation.54 | convolution fusion | flops 1073741824 | bytes 6815744 | tf_op jit(solution)/shard_map/dot_general | solution.py:87
  12.5 4.3 %fusion.39 = f32[512,256]{0,1:T(8,128)} fusion(bf16[512,4096]{1,0:T(8,128)(2,1)} %param.11, bf16[4096,256]{1,0:T(8,128)(2,1)S(1)} %copy-done), kind=kOutput, calls=%fused_computation.53 | convolution fusion | flops 1073741824 | bytes 6815744 | tf_op jit(solution)/shard_map/dot_general | solution.py:86
  18.2 18.7 %reduce-scatter.5.cloned.1.call-done = f32[512,64]{0,1:T(8,128)} async-done(((f32[512,256]{0,1:T(8,128)}), f32[512,64]{0,1:T(8,128)}) %reduce-scatter.5.cloned.1.call-update) | async-done | bytes 131088 | tf_op jit(solution)/shard_map/reduce_scatter | solution.py:90
  36.9 0.9 multiply_convert_fusion.4
  37.9 23.9 %reduce-scatter.3.cloned.1.call-done = f32[512,64]{0,1:T(8,128)} async-done(((f32[512,256]{0,1:T(8,128)}), f32[512,64]{0,1:T(8,128)}) %reduce-scatter.3.cloned.1.call-update) | async-done | bytes 131088 | tf_op jit(solution)/shard_map/reduce_scatter | solution.py:89
  61.7 1.6 multiply_convert_fusion.5
  63.3 1.0 maximum_select_fusion.1
  65.0 1.0 maximum_select_fusion
  66.8 70.5 %while.16 = (s32[]{:T(128)}, f32[512,128]{1,0:T(8,128)}, f32[512,128]{1,0:T(8,128)S(1)}, bf16[512,1024]{1,0:T(8,128)(2,1)}, bf16[512,128]{1,0:T(8,128)(2,1)}, /*...) while((s32[]{:T(128)}, f32[512,128]{1,0:T(8,128)}, ...), condition=%wide.region_7.8_spmd.clone, body=%wide.region_3.7_spmd.clone.sunk | while | flops 340261376 | bytes 11557142 | solution.py:115
  66.8 0.9 constant_dynamic-slice_fusion.2
  68.5 1.4 fusion.77
  70.2 0.8 copy-done.1
  71.0 0.9 fusion.80
  71.9 2.2 %fusion.81 = f32[512,128]{1,0:T(8,128)} fusion(bf16[512,128]{1,0:T(8,128)(2,1)} %get-tuple-element.304, bf16[512,128]{1,0:T(8,128)(2,1)S(1)} %constant_dynamic-slice_fusion.2, f32[512]{0:T(512)} %fusion.80, f32[512,512]{0,1:T(8,128)S(1)} %get-tuple-element.272, f32[512]{0:T(512)S(1)} %fusion.78, f32[512]{0:T(512)S(1)} %get-tuple-element.273, ...), kind=kOutput, calls=%fused_computation.8.clone.1 | convolution fusion | flops 135725056 | bytes 1972229 | tf_op jit(solution)/shard_map/while/body/eval_jaxpr/dot_general | solution.py:48
  74.1 1.4 convolution_add_fusion.2
  75.5 0.9 constant_dynamic-slice_fusion.2
  77.2 1.4 fusion.77
  78.9 0.8 copy-done.1
  79.7 0.9 fusion.80
  80.6 2.4 %fusion.81 = f32[512,128]{1,0:T(8,128)} fusion(bf16[512,128]{1,0:T(8,128)(2,1)} %get-tuple-element.304, bf16[512,128]{1,0:T(8,128)(2,1)S(1)} %constant_dynamic-slice_fusion.2, f32[512]{0:T(512)} %fusion.80, f32[512,512]{0,1:T(8,128)S(1)} %get-tuple-element.272, f32[512]{0:T(512)S(1)} %fusion.78, f32[512]{0:T(512)S(1)} %get-tuple-element.273, ...), kind=kOutput, calls=%fused_computation.8.clone.1 | convolution fusion | flops 135725056 | bytes 1972229 | tf_op jit(solution)/shard_map/while/body/eval_jaxpr/dot_general | solution.py:48
  82.9 1.4 convolution_add_fusion.2
  84.3 0.9 constant_dynamic-slice_fusion.2
  86.0 1.4 fusion.77
  87.8 0.8 copy-done.1
  88.5 0.9 fusion.80
  89.4 2.4 %fusion.81 = f32[512,128]{1,0:T(8,128)} fusion(bf16[512,128]{1,0:T(8,128)(2,1)} %get-tuple-element.304, bf16[512,128]{1,0:T(8,128)(2,1)S(1)} %constant_dynamic-slice_fusion.2, f32[512]{0:T(512)} %fusion.80, f32[512,512]{0,1:T(8,128)S(1)} %get-tuple-element.272, f32[512]{0:T(512)S(1)} %fusion.78, f32[512]{0:T(512)S(1)} %get-tuple-element.273, ...), kind=kOutput, calls=%fused_computation.8.clone.1 | convolution fusion | flops 135725056 | bytes 1972229 | tf_op jit(solution)/shard_map/while/body/eval_jaxpr/dot_general | solution.py:48
  91.8 1.4 convolution_add_fusion.2
  93.1 0.9 constant_dynamic-slice_fusion.2
  94.8 1.4 fusion.77
  96.6 0.8 copy-done.1
  97.4 0.9 fusion.80
  98.2 2.4 %fusion.81 = f32[512,128]{1,0:T(8,128)} fusion(bf16[512,128]{1,0:T(8,128)(2,1)} %get-tuple-element.304, bf16[512,128]{1,0:T(8,128)(2,1)S(1)} %constant_dynamic-slice_fusion.2, f32[512]{0:T(512)} %fusion.80, f32[512,512]{0,1:T(8,128)S(1)} %get-tuple-element.272, f32[512]{0:T(512)S(1)} %fusion.78, f32[512]{0:T(512)S(1)} %get-tuple-element.273, ...), kind=kOutput, calls=%fused_computation.8.clone.1 | convolution fusion | flops 135725056 | bytes 1972229 | tf_op jit(solution)/shard_map/while/body/eval_jaxpr/dot_general | solution.py:48
  100.6 1.4 convolution_add_fusion.2
  102.0 0.9 constant_dynamic-slice_fusion.2
  103.7 1.4 fusion.77
  106.2 0.9 fusion.80
  107.1 2.4 %fusion.81 = f32[512,128]{1,0:T(8,128)} fusion(bf16[512,128]{1,0:T(8,128)(2,1)} %get-tuple-element.304, bf16[512,128]{1,0:T(8,128)(2,1)S(1)} %constant_dynamic-slice_fusion.2, f32[512]{0:T(512)} %fusion.80, f32[512,512]{0,1:T(8,128)S(1)} %get-tuple-element.272, f32[512]{0:T(512)S(1)} %fusion.78, f32[512]{0:T(512)S(1)} %get-tuple-element.273, ...), kind=kOutput, calls=%fused_computation.8.clone.1 | convolution fusion | flops 135725056 | bytes 1972229 | tf_op jit(solution)/shard_map/while/body/eval_jaxpr/dot_general | solution.py:48
  109.4 1.4 convolution_add_fusion.2
  110.8 0.9 constant_dynamic-slice_fusion.2
  112.5 1.4 fusion.77
  115.0 0.9 fusion.80
  115.9 2.4 %fusion.81 = f32[512,128]{1,0:T(8,128)} fusion(bf16[512,128]{1,0:T(8,128)(2,1)} %get-tuple-element.304, bf16[512,128]{1,0:T(8,128)(2,1)S(1)} %constant_dynamic-slice_fusion.2, f32[512]{0:T(512)} %fusion.80, f32[512,512]{0,1:T(8,128)S(1)} %get-tuple-element.272, f32[512]{0:T(512)S(1)} %fusion.78, f32[512]{0:T(512)S(1)} %get-tuple-element.273, ...), kind=kOutput, calls=%fused_computation.8.clone.1 | convolution fusion | flops 135725056 | bytes 1972229 | tf_op jit(solution)/shard_map/while/body/eval_jaxpr/dot_general | solution.py:48
  118.3 1.4 convolution_add_fusion.2
  119.7 0.9 constant_dynamic-slice_fusion.2
  121.3 1.4 fusion.77
  123.9 0.9 fusion.80
  124.7 2.4 %fusion.81 = f32[512,128]{1,0:T(8,128)} fusion(bf16[512,128]{1,0:T(8,128)(2,1)} %get-tuple-element.304, bf16[512,128]{1,0:T(8,128)(2,1)S(1)} %constant_dynamic-slice_fusion.2, f32[512]{0:T(512)} %fusion.80, f32[512,512]{0,1:T(8,128)S(1)} %get-tuple-element.272, f32[512]{0:T(512)S(1)} %fusion.78, f32[512]{0:T(512)S(1)} %get-tuple-element.273, ...), kind=kOutput, calls=%fused_computation.8.clone.1 | convolution fusion | flops 135725056 | bytes 1972229 | tf_op jit(solution)/shard_map/while/body/eval_jaxpr/dot_general | solution.py:48
  127.1 1.4 convolution_add_fusion.2
  128.5 0.9 constant_dynamic-slice_fusion.2
  130.2 1.4 fusion.77
  131.9 0.8 copy-done.1
  132.7 0.9 fusion.80
  133.6 2.4 %fusion.81 = f32[512,128]{1,0:T(8,128)} fusion(bf16[512,128]{1,0:T(8,128)(2,1)} %get-tuple-element.304, bf16[512,128]{1,0:T(8,128)(2,1)S(1)} %constant_dynamic-slice_fusion.2, f32[512]{0:T(512)} %fusion.80, f32[512,512]{0,1:T(8,128)S(1)} %get-tuple-element.272, f32[512]{0:T(512)S(1)} %fusion.78, f32[512]{0:T(512)S(1)} %get-tuple-element.273, ...), kind=kOutput, calls=%fused_computation.8.clone.1 | convolution fusion | flops 135725056 | bytes 1972229 | tf_op jit(solution)/shard_map/while/body/eval_jaxpr/dot_general | solution.py:48
  135.9 1.4 convolution_add_fusion.2
  137.3 1.0 convert.7
  139.1 17.2 %all-gather.2.cloned.1.call-done = bf16[512,1024]{1,0:T(8,128)(2,1)} async-done(((bf16[512,256]{1,0:T(8,128)(2,1)}), bf16[512,1024]{1,0:T(8,128)(2,1)}) %all-gather.2.cloned.1.call-update) | async-done | bytes 1048592 | tf_op jit(solution)/shard_map/all_gather | solution.py:117
  156.2 4.1 %reshape.20 = f32[512,2,2,2,128]{4,3,2,1,0:T(2,128)} reshape(bf16[512,1024]{1,0:T(8,128)(2,1)} %all-gather.2.cloned.1.call-done) | data formatting | bytes 3145728 | tf_op jit(solution)/shard_map/reshape | solution.py:120
  160.3 3.9 %reduce_sum.45 = f32[512,2,2,128]{3,2,1,0:T(2,128)S(1)} reduce(f32[512,2,2,2,128]{4,3,2,1,0:T(2,128)} %reshape.20, f32[]{:T(128)} %constant.72.clone.1), dimensions={2}, to_apply=%region_8.9 | reduce | flops 262144 | bytes 3145732 | tf_op jit(solution)/shard_map/reduce_sum | solution.py:121
  164.2 1.8 fusion.38
  166.0 2.0 copy.23
  168.0 1.2 copy.22
  169.3 1.3 fusion.19
  171.2 3.3 %add_convert_fusion = bf16[512,4096]{1,0:T(8,128)(2,1)} fusion(f32[512,4096]{1,0:T(8,128)S(1)} %fusion.19, bf16[4096,256]{1,0:T(8,128)(2,1)S(1)} %copy-done.8, f32[512,256]{0,1:T(8,128)S(1)} %bitcast.35, f32[512,256]{0,1:T(8,128)S(1)} %copy-done.4), kind=kOutput, calls=%fused_computation.24 | convolution fusion | flops 1078198272 | bytes 15728640 | tf_op jit(solution)/shard_map/dot_general | solution.py:57
  175.2 37.7 %all-reduce = (f32[32,64]{1,0:T(8,128)}, f32[32,64]{1,0:T(8,128)}) all-reduce(f32[32,64]{1,0:T(8,128)S(1)} %fusion.25, f32[32,64]{1,0:T(8,128)S(1)} %fusion.23), channel_id=1, replica_groups=mesh['dp'=8,'tensor'=4] {'dp'}, use_global_device_ids=true, to_apply=%region_9.10 | all-reduce | flops 4096 | bytes 32768 | tf_op jit(solution)/shard_map/psum | solution.py:141
  (116 shorter events, 16.7 us)
Async XLA Ops:
  7.2 5.3 %copy-start = (bf16[4096,256]{1,0:T(8,128)(2,1)S(1)}, bf16[4096,256]{1,0:T(8,128)(2,1)}, u32[]{:S(2)}) copy-start(bf16[4096,256]{1,0:T(8,128)(2,1)} %param.14) | copy-start | bytes 6291460
  7.2 29.7 %reduce-scatter.5.cloned.1.call-start = ((), (), s32[]{:S(2)}) async-start(), calls=%async_computation.3 | async-start | bytes 655360 | tf_op jit(solution)/shard_map/reduce_scatter | solution.py:90
  12.3 4.7 %copy-start.15 = (s32[1,512]{1,0:T(1,128)S(1)}, s32[1,512]{1,0:T(1,128)}, u32[]{:S(2)}) copy-start(s32[1,512]{1,0:T(1,128)} %param.18) | copy-start | bytes 6148
  12.4 4.7 %copy-start.16 = (s32[1,4]{1,0:T(1,128)S(1)}, s32[1,4]{1,0:T(1,128)}, u32[]{:S(2)}) copy-start(s32[1,4]{1,0:T(1,128)} %param.19) | copy-start | bytes 52
  12.4 4.8 %copy-start.13 = (f32[32,256]{1,0:T(8,128)S(1)}, f32[32,256]{1,0:T(8,128)}, u32[]{:S(2)}) copy-start(f32[32,256]{1,0:T(8,128)} %param.17) | copy-start | bytes 98308
  12.4 5.3 %copy-start.14 = (f32[32,256]{1,0:T(8,128)S(1)}, f32[32,256]{1,0:T(8,128)}, u32[]{:S(2)}) copy-start(f32[32,256]{1,0:T(8,128)} %param.16) | copy-start | bytes 98308
  12.4 49.3 %reduce-scatter.3.cloned.1.call-start = ((), (), s32[]{:S(2)}) async-start(), calls=%async_computation.2 | async-start | bytes 655360 | tf_op jit(solution)/shard_map/reduce_scatter | solution.py:89
  16.8 139.5 %all-gather.2.cloned.1.call-start = ((), (), s32[]{:S(2)}) async-start(), calls=%async_computation.4 | async-start | bytes 1310720 | tf_op jit(solution)/shard_map/all_gather | solution.py:117
  17.7 49.1 %copy-start.3 = (f32[512,256]{0,1:T(8,128)}, f32[512,256]{0,1:T(8,128)S(1)}, u32[]{:S(2)}) copy-start(f32[512,256]{0,1:T(8,128)S(1)} %fusion.21) | copy-start | bytes 1572868
  18.2 48.6 %copy-start.5 = (f32[512,256]{0,1:T(8,128)}, f32[512,256]{0,1:T(8,128)S(1)}, u32[]{:S(2)}) copy-start(f32[512,256]{0,1:T(8,128)S(1)} %fusion.22) | copy-start | bytes 1572868
  37.8 25.5 %copy-start.11 = (bf16[512,64]{0,1:T(8,128)(2,1)}, bf16[512,64]{0,1:T(8,128)(2,1)S(1)}, u32[]{:S(2)}) copy-start(bf16[512,64]{0,1:T(8,128)(2,1)S(1)} %multiply_convert_fusion.4) | copy-start | bytes 196612
  37.8 25.5 %collective-permute-start.1 = (bf16[512,64]{0,1:T(8,128)(2,1)S(1)}, bf16[512,64]{0,1:T(8,128)(2,1)}, u32[]{:S(2)}, u32[]{:S(2)}) collective-permute-start(bf16[512,64]{0,1:T(8,128)(2,1)S(1)} %multiply_convert_fusion.4), channel_id=1, source_target_pairs={{0,1},{1,0},{2,3},{3,2},{4,5},{5,4},{6,7},{7,6},{8,9},{9,8},{10,11... | collective-permute-start | bytes 196616 | tf_op jit(solution)/shard_map/ppermute | solution.py:11
  63.3 1.8 collective-permute-start
  68.5 2.5 %copy-start.2 = (bf16[512,128]{0,1:T(8,128)(2,1)S(1)}, bf16[512,128]{0,1:T(8,128)(2,1)}, u32[]{:S(2)}) copy-start(bf16[512,128]{0,1:T(8,128)(2,1)} %copy.27) | copy-start | bytes 393220 | tf_op jit(solution)/shard_map/while
  68.5 2.5 %copy-start.12 = (bf16[512,128]{1,0:T(8,128)(2,1)S(1)}, bf16[512,128]{1,0:T(8,128)(2,1)}, u32[]{:S(2)}) copy-start(bf16[512,128]{1,0:T(8,128)(2,1)} %get-tuple-element.304) | copy-start | bytes 393220 | tf_op jit(solution)/shard_map/while
  70.2 0.8 copy-start.1
  77.2 2.5 %copy-start.2 = (bf16[512,128]{0,1:T(8,128)(2,1)S(1)}, bf16[512,128]{0,1:T(8,128)(2,1)}, u32[]{:S(2)}) copy-start(bf16[512,128]{0,1:T(8,128)(2,1)} %copy.27) | copy-start | bytes 393220 | tf_op jit(solution)/shard_map/while
  77.2 2.5 %copy-start.12 = (bf16[512,128]{1,0:T(8,128)(2,1)S(1)}, bf16[512,128]{1,0:T(8,128)(2,1)}, u32[]{:S(2)}) copy-start(bf16[512,128]{1,0:T(8,128)(2,1)} %get-tuple-element.304) | copy-start | bytes 393220 | tf_op jit(solution)/shard_map/while
  78.9 0.8 copy-start.1
  86.0 2.5 %copy-start.2 = (bf16[512,128]{0,1:T(8,128)(2,1)S(1)}, bf16[512,128]{0,1:T(8,128)(2,1)}, u32[]{:S(2)}) copy-start(bf16[512,128]{0,1:T(8,128)(2,1)} %copy.27) | copy-start | bytes 393220 | tf_op jit(solution)/shard_map/while
  86.0 2.5 %copy-start.12 = (bf16[512,128]{1,0:T(8,128)(2,1)S(1)}, bf16[512,128]{1,0:T(8,128)(2,1)}, u32[]{:S(2)}) copy-start(bf16[512,128]{1,0:T(8,128)(2,1)} %get-tuple-element.304) | copy-start | bytes 393220 | tf_op jit(solution)/shard_map/while
  87.7 0.8 copy-start.1
  94.8 2.5 %copy-start.2 = (bf16[512,128]{0,1:T(8,128)(2,1)S(1)}, bf16[512,128]{0,1:T(8,128)(2,1)}, u32[]{:S(2)}) copy-start(bf16[512,128]{0,1:T(8,128)(2,1)} %copy.27) | copy-start | bytes 393220 | tf_op jit(solution)/shard_map/while
  94.8 2.5 %copy-start.12 = (bf16[512,128]{1,0:T(8,128)(2,1)S(1)}, bf16[512,128]{1,0:T(8,128)(2,1)}, u32[]{:S(2)}) copy-start(bf16[512,128]{1,0:T(8,128)(2,1)} %get-tuple-element.304) | copy-start | bytes 393220 | tf_op jit(solution)/shard_map/while
  96.6 0.8 copy-start.1
  103.7 2.5 %copy-start.2 = (bf16[512,128]{0,1:T(8,128)(2,1)S(1)}, bf16[512,128]{0,1:T(8,128)(2,1)}, u32[]{:S(2)}) copy-start(bf16[512,128]{0,1:T(8,128)(2,1)} %copy.27) | copy-start | bytes 393220 | tf_op jit(solution)/shard_map/while
  103.7 2.5 %copy-start.12 = (bf16[512,128]{1,0:T(8,128)(2,1)S(1)}, bf16[512,128]{1,0:T(8,128)(2,1)}, u32[]{:S(2)}) copy-start(bf16[512,128]{1,0:T(8,128)(2,1)} %get-tuple-element.304) | copy-start | bytes 393220 | tf_op jit(solution)/shard_map/while
  105.4 0.8 copy-start.1
  112.5 2.5 %copy-start.2 = (bf16[512,128]{0,1:T(8,128)(2,1)S(1)}, bf16[512,128]{0,1:T(8,128)(2,1)}, u32[]{:S(2)}) copy-start(bf16[512,128]{0,1:T(8,128)(2,1)} %copy.27) | copy-start | bytes 393220 | tf_op jit(solution)/shard_map/while
  112.5 2.5 %copy-start.12 = (bf16[512,128]{1,0:T(8,128)(2,1)S(1)}, bf16[512,128]{1,0:T(8,128)(2,1)}, u32[]{:S(2)}) copy-start(bf16[512,128]{1,0:T(8,128)(2,1)} %get-tuple-element.304) | copy-start | bytes 393220 | tf_op jit(solution)/shard_map/while
  114.2 0.8 copy-start.1
  121.3 2.5 %copy-start.2 = (bf16[512,128]{0,1:T(8,128)(2,1)S(1)}, bf16[512,128]{0,1:T(8,128)(2,1)}, u32[]{:S(2)}) copy-start(bf16[512,128]{0,1:T(8,128)(2,1)} %copy.27) | copy-start | bytes 393220 | tf_op jit(solution)/shard_map/while
  121.3 2.5 %copy-start.12 = (bf16[512,128]{1,0:T(8,128)(2,1)S(1)}, bf16[512,128]{1,0:T(8,128)(2,1)}, u32[]{:S(2)}) copy-start(bf16[512,128]{1,0:T(8,128)(2,1)} %get-tuple-element.304) | copy-start | bytes 393220 | tf_op jit(solution)/shard_map/while
  123.1 0.8 copy-start.1
  130.2 2.5 %copy-start.2 = (bf16[512,128]{0,1:T(8,128)(2,1)S(1)}, bf16[512,128]{0,1:T(8,128)(2,1)}, u32[]{:S(2)}) copy-start(bf16[512,128]{0,1:T(8,128)(2,1)} %copy.27) | copy-start | bytes 393220 | tf_op jit(solution)/shard_map/while
  130.2 2.5 %copy-start.12 = (bf16[512,128]{1,0:T(8,128)(2,1)S(1)}, bf16[512,128]{1,0:T(8,128)(2,1)}, u32[]{:S(2)}) copy-start(bf16[512,128]{1,0:T(8,128)(2,1)} %get-tuple-element.304) | copy-start | bytes 393220 | tf_op jit(solution)/shard_map/while
  131.9 0.8 copy-start.1
  166.0 3.3 %copy-start.6 = (f32[512,256]{0,1:T(8,128)S(1)}, f32[512,256]{0,1:T(8,128)}, u32[]{:S(2)}) copy-start(f32[512,256]{0,1:T(8,128)} %copy-done.5) | copy-start | bytes 1572868
  169.2 1.3 copy-start.4
  169.2 1.3 copy-start.7
  169.3 1.9 copy-start.8
  171.2 3.3 %copy-start.9 = (f32[512,64]{0,1:T(8,128)S(1)}, f32[512,64]{0,1:T(8,128)}, u32[]{:S(2)}) copy-start(f32[512,64]{0,1:T(8,128)} %reduce-scatter.5.cloned.1.call-done) | copy-start | bytes 393220
  171.2 3.7 %copy-start.10 = (f32[512,64]{0,1:T(8,128)S(1)}, f32[512,64]{0,1:T(8,128)}, u32[]{:S(2)}) copy-start(f32[512,64]{0,1:T(8,128)} %reduce-scatter.3.cloned.1.call-done) | copy-start | bytes 393220
Sparse Core Ops, SparseCore 0:
  12.5 24.3 reduce-scatter.4
  40.1 21.6 reduce-scatter.2
  139.2 16.9 all-gather.1
where the time goes:
time: 221 us; the launch traced here: 219 us
  matrix products  63.1 us (29%)
  waiting for transfers between devices  59.7 us (27%)
  blocking collectives  37.7 us (17%)
  local copies, waits for them, and re-layouts  31.1 us (14%)
  between operations  14 us (6%)
  other arithmetic  13 us (6%)
    psum x1, blocking collectives, on_device(): key_total, value_total = lax.psum((key_tenant, value_tenant), 'dp')  37.7 us
    reduce_scatter x1, waiting for transfers between devices, on_device(): lax.psum_scatter(key_partial_sum, 'tensor', scatter_dimension=1, tiled=True)  23.9 us
    dot_general x8, matrix products, head_grads(): lax.dot_general(score_grad, query_head, (((0,), (0,)), ((), ())), preferr...  18.7 us
    reduce_scatter x1, waiting for transfers between devices, on_device(): lax.psum_scatter(value_partial_sum, 'tensor', scatter_dimension=1, tiled=...  18.7 us
    all_gather x1, waiting for transfers between devices, on_device(): lax.all_gather(partials.astype(jnp.bfloat16), 'tensor', axis=1, tiled=True)  17.2 us
    dynamic_slice x16, local copies, waits for them, and re-layouts, one_head(): out_head = lax.dynamic_slice_in_dim(out_grad, column, head_width, 1)  13.5 us
    dot_general x8, matrix products, head_grads(): lax.dot_general(query_head, key_tile, (((1,), (1,)), ((), ())), preferred...  10.9 us
    dot_general x8, matrix products, head_grads(): lax.dot_general(probs_low, out_head, (((0,), (0,)), ((), ())), preferred_...  10.8 us
  transfers between devices with their start and end apart: 5, of which 3 were waited for; matrix products, arithmetic and copies ran while one was open for 4% of the time, Pallas kernels for 0%

commit v1 on v0

v1 whole, which is shorter than its diff:
```python
import functools
import math

import jax
import jax.numpy as jnp
from jax import lax
from jax.experimental import pallas as pl
from jax.experimental.pallas import tpu as pltpu
from jax.sharding import PartitionSpec as P

MESH = pl.DeviceIdType.MESH
F32 = jnp.float32
BF16 = jnp.bfloat16
SEQS = 4
NT = 32
HD = 128
RB = 128
LONGEST = 256
VMEM_LIMIT = 48 * 1024 * 1024
KC = 4


def dot_nt(a, b):
    return lax.dot_general(a, b, (((1,), (1,)), ((), ())), preferred_element_type=F32)


def dot_nn(a, b):
    return jnp.dot(a, b, preferred_element_type=F32)


def inner(
    ndp, nten, tok_hbm, q_hbm, o_hbm, kw_hbm, vw_hbm, ks, vs, seg, tenants,
    low_out, sums_out,
    tok, q, o, kw, vw, part, from_core, from_chip, base, kv, factor, bias, grads, grads_in, lows, sums,
    sem_w, sem_t, sem_q, sem_o,
    s1, r1, s2, r2, s3, r3, s4, r4, s5, r5, s6, r6, s7, r7, sg, rg,
):
    chips = nten // 2
    rows_all, depth = tok.shape
    nb = rows_all // RB
    look = LONGEST // RB
    half = rows_all // 2
    kc = depth // KC
    d = lax.axis_index("dp")
    t = lax.axis_index("tensor")
    x = t // 2
    c = lax.rem(t, 2)
    other = 1 - c
    cf = c.astype(F32)
    partner = (d, 2 * x + other)
    peers = [(d, 2 * lax.rem(x + p, chips) + c) for p in range(1, chips)]
    groups = [lax.rem(d + i, ndp) for i in range(ndp)]

    def rows(b):
        return pl.ds(b * RB, RB)

    loads = {}
    for k in range(KC):
        ks_ = pl.ds(k * kc, kc)
        loads["k", k] = pltpu.make_async_copy(kw_hbm.at[ks_], kw.at[ks_], sem_w.at[k])
        loads["v", k] = pltpu.make_async_copy(vw_hbm.at[ks_], vw.at[ks_], sem_w.at[KC + k])
        loads["t", 0, k] = pltpu.make_async_copy(
            tok_hbm.at[pl.ds(0, half), ks_], tok.at[pl.ds(0, half), ks_], sem_t.at[k])
        loads["t", 1, k] = pltpu.make_async_copy(
            tok_hbm.at[pl.ds(half, half), ks_], tok.at[pl.ds(half, half), ks_], sem_t.at[KC + k])
    for b in range(nb):
        loads["q", b] = pltpu.make_async_copy(q_hbm.at[rows(b)], q.at[rows(b)], sem_q.at[b])
        loads["o", b] = pltpu.make_async_copy(o_hbm.at[rows(b)], o.at[rows(b)], sem_o.at[b])
    for k in range(KC):
        loads["k", k].start()
        loads["v", k].start()
        loads["t", 0, k].start()
    for k in range(KC):
        loads["t", 1, k].start()
    for b in range(nb):
        loads["q", b].start()
        loads["o", b].start()

    barrier = pltpu.get_barrier_semaphore()
    count = 0
    for dev in [partner] + peers:
        pl.semaphore_signal(barrier, inc=1, device_id=dev, device_id_type=MESH)
        count += 1
    for i in range(1, ndp):
        for core in range(2):
            pl.semaphore_signal(barrier, inc=1, device_id=(groups[i], 2 * x + core), device_id_type=MESH)
            count += 1

    def send(src, dst, ssem, rsem, dev):
        copy = pltpu.make_async_remote_copy(
            src_ref=src, dst_ref=dst, send_sem=ssem, recv_sem=rsem, device_id=dev, device_id_type=MESH)
        copy.start()
        return copy

    def arrived(dst, rsem):
        pltpu.make_async_remote_copy(
            src_ref=dst, dst_ref=dst, send_sem=s1.at[0], recv_sem=rsem, device_id=partner, device_id_type=MESH
        ).wait_recv()

    sent = []

    segments = seg[...]
    counts = [jnp.sum(jnp.where(segments == s, 1.0, 0.0), axis=1, keepdims=True) for s in range(SEQS)]
    bounds = [jnp.zeros((1, 1), F32)]
    for s in range(SEQS):
        bounds.append(bounds[-1] + counts[s])
    start = jnp.zeros(segments.shape, F32)
    for s in range(1, SEQS):
        start = jnp.where(segments == s, bounds[s], start)
    own_cols = pl.ds(pl.multiple_of(x * HD, HD), HD)
    own_scale = ks[:, own_cols] * (1.0 - cf) + vs[:, own_cols] * cf
    tenant = lax.broadcasted_iota(jnp.int32, (NT, HD), 0)
    scale_rows = [
        jnp.sum(jnp.where(tenant == tenants[0, s], own_scale, 0.0), axis=0, keepdims=True) for s in range(SEQS)]

    def position(b):
        return lax.broadcasted_iota(jnp.int32, (RB, HD), 0).astype(F32) + float(b * RB)

    for b in range(nb):
        pos = position(b)
        f = jnp.broadcast_to(scale_rows[SEQS - 1], (RB, HD))
        for s in range(SEQS - 2, -1, -1):
            f = jnp.where(pos < bounds[s + 1], scale_rows[s], f)
        factor[rows(b), :] = f
        grads[0, rows(b), :] = jnp.zeros((RB, HD), F32)
        grads[1, rows(b), :] = jnp.zeros((RB, HD), F32)

    pl.semaphore_wait(barrier, count)

    def project(r):
        rr = pl.ds(r * half, half)
        for k in range(KC):
            kk = pl.ds(k * kc, kc)
            if r == 0:
                loads["k", k].wait()
                loads["v", k].wait()
            loads["t", r, k].wait()
            block = tok[rr, kk]
            for kind, weight in ((0, kw), (1, vw)):
                value = dot_nn(block, weight[kk, :])
                for h in range(chips):
                    piece = value[:, h * HD:(h + 1) * HD]
                    if k:
                        piece = piece + part[kind, h, rr, :]
                    part[kind, h, rr, :] = piece

    def to_core(b):
        sent.append(send(part.at[other, :, rows(b)], from_core.at[:, rows(b)], s1.at[b], r1.at[b], partner))

    def to_chips(b):
        arrived(from_core.at[:, rows(b)], r1.at[b])
        for p in range(1, chips):
            j = lax.rem(x + p, chips)
            part[c, j, rows(b), :] = part[c, j, rows(b), :] + from_core[j, rows(b), :]
            i = (p - 1) * nb + b
            sent.append(send(part.at[c, j, rows(b)], from_chip.at[p - 1, rows(b)], s2.at[i], r2.at[i], peers[p - 1]))

    def finish(b):
        total = part[c, x, rows(b), :] + from_core[x, rows(b), :]
        for p in range(1, chips):
            arrived(from_chip.at[p - 1, rows(b)], r2.at[(p - 1) * nb + b])
            total = total + from_chip[p - 1, rows(b), :]
        base[rows(b), :] = total
        kv[c, rows(b), :] = (total * factor[rows(b), :]).astype(BF16)
        sent.append(send(kv.at[c, rows(b)], kv.at[c, rows(b)], s3.at[b], r3.at[b], partner))

    heads = q.shape[1] // HD
    score_scale = HD ** -0.5
    to_exp2 = score_scale * math.log2(math.e)

    def ready(b):
        arrived(kv.at[other, rows(b)], r3.at[b])
        loads["q", b].wait()
        loads["o", b].wait()
        first = max(0, b - look)
        query_pos = lax.broadcasted_iota(jnp.int32, (RB, RB), 1).astype(F32) + float(b * RB)
        begin = start[:, b * RB:(b + 1) * RB]
        for j in range(first, b + 1):
            key_pos = position(j)
            seen = (key_pos >= begin) & (key_pos <= query_pos)
            bias[rows(j - first), :] = jnp.where(seen, 0.0, -1e30)

    def attend(b, lo, hi):
        first = max(0, b - look)
        width = (b + 1 - first) * RB
        keys_at = pl.ds(first * RB, width)

        def pair(i, _):
            c0 = pl.multiple_of(i * 2 * HD, 2 * HD)
            c1 = pl.multiple_of(i * 2 * HD + HD, HD)
            qh = jnp.concatenate([q[rows(b), pl.ds(c0, HD)], q[rows(b), pl.ds(c1, HD)]], axis=0)
            oh = jnp.concatenate([o[rows(b), pl.ds(c0, HD)], o[rows(b), pl.ds(c1, HD)]], axis=0)
            hidden = bias[pl.ds(0, width), :]
            scores = dot_nt(kv[0, keys_at, :], qh) + jnp.concatenate([hidden, hidden], axis=1)
            grad = dot_nt(kv[1, keys_at, :], oh)
            peak = jnp.max(scores, axis=0, keepdims=True)
            e = jnp.exp2((scores - peak) * to_exp2)
            probs = e * (1.0 / jnp.sum(e, axis=0, keepdims=True))
            low = probs.astype(BF16)
            delta = jnp.sum(low.astype(F32) * grad, axis=0, keepdims=True)
            score_grad = (probs * (grad - delta)).astype(BF16)
            grads[1, keys_at, :] = grads[1, keys_at, :] + dot_nn(low, oh)
            grads[0, keys_at, :] = grads[0, keys_at, :] + dot_nn(score_grad, qh)
            return 0

        lax.fori_loop(lo, hi, pair, 0)

    def grads_to_core(b):
        sent.append(send(grads.at[other, rows(b)], grads_in.at[rows(b)], s4.at[b], r4.at[b], partner))

    tables = [jnp.zeros((1, HD), F32) for s in range(SEQS)]

    def lows_out(b):
        arrived(grads_in.at[rows(b)], r4.at[b])
        total = (grads[c, rows(b), :] + grads_in[rows(b), :]) * (cf + (1.0 - cf) * score_scale)
        lows[c, x, rows(b), :] = (total * factor[rows(b), :]).astype(BF16)
        for p in range(1, chips):
            i = (p - 1) * nb + b
            sent.append(send(lows.at[c, x, rows(b)], lows.at[c, x, rows(b)], s6.at[i], r6.at[i], peers[p - 1]))
        sent.append(send(lows.at[c, x, rows(b)], lows.at[c, x, rows(b)], s5.at[b], r5.at[b], partner))
        product = total * base[rows(b), :]
        pos = position(b)
        for s in range(SEQS):
            inside = (pos >= bounds[s]) & (pos < bounds[s + 1])
            tables[s] = tables[s] + jnp.sum(jnp.where(inside, product, 0.0), axis=0, keepdims=True)

    def forward(b):
        for p in range(1, chips):
            j = lax.rem(x + chips - p, chips)
            i = (p - 1) * nb + b
            arrived(lows.at[c, j, rows(b)], r6.at[i])
            sent.append(send(lows.at[c, j, rows(b)], lows.at[c, j, rows(b)], s7.at[i], r7.at[i], partner))

    for r in range(2):
        project(r)
        for b in range(r * nb // 2, (r + 1) * nb // 2):
            to_core(b)
        if r == 0:
            for b in range(nb // 2):
                to_chips(b)
    for b in range(nb // 2, nb):
        to_chips(b)
    finish(0)
    finish(1)
    pairs = heads // 2
    for b in range(nb):
        ready(b)
        last = b == nb - 1
        attend(b, 0, pairs // 2 if last else pairs)
        if b + 2 < nb:
            finish(b + 2)
        if last:
            for j in range(nb - 1 - look):
                lows_out(j)
            attend(b, pairs // 2, pairs)
        elif b >= look:
            grads_to_core(b - look)
    for j in range(nb - 1 - look, nb):
        grads_to_core(j)
    for j in range(nb - 1 - look, nb):
        lows_out(j)

    for s in range(SEQS):
        sums[0, c, pl.ds(s, 1), :] = tables[s]
        sums[0, c, pl.ds(SEQS + s, 1), :] = jnp.full((1, HD), 1.0, F32) * tenants[0, s].astype(F32)
    for i in range(ndp):
        if i == 0:
            sent.append(send(sums.at[0, c], sums.at[0, c], sg.at[other], rg.at[c], partner))
        else:
            for core in range(2):
                sent.append(send(
                    sums.at[0, c], sums.at[i, c], sg.at[2 * i + core], rg.at[2 * i + c], (groups[i], 2 * x + core)))
    for b in range(nb):
        forward(b)
    for b in range(nb):
        arrived(lows.at[other, x, rows(b)], r5.at[b])
        for p in range(1, chips):
            j = lax.rem(x + chips - p, chips)
            arrived(lows.at[other, j, rows(b)], r7.at[(p - 1) * nb + b])
    for kind in range(2):
        for h in range(chips):
            low_out[:, pl.ds((kind * chips + h) * HD, HD)] = lows[kind, h]
    for i in range(ndp):
        if i == 0:
            arrived(sums.at[0, other], rg.at[other])
        else:
            for core in range(2):
                arrived(sums.at[i, core], rg.at[2 * i + core])
    for i in range(ndp):
        for core in range(2):
            value = sums[i, core]
            turned = jnp.concatenate([value[:, HD // 2:], value[:, :HD // 2]], axis=1)
            sums_out[i, core] = value * (1.0 - cf) + turned * cf
    for copy in sent:
        copy.wait_send()


def closing(ndp, low, kw, vw, sums, grad_out, key_out, value_out):
    wide = kw.shape[1]
    grad = dot_nt(low[:, :wide], kw[...]) + dot_nt(low[:, wide:], vw[...])
    grad_out[...] = grad.astype(BF16)

    @pl.when(pl.program_id(0) == 0)
    def _():
        tenant = lax.broadcasted_iota(jnp.int32, (NT, HD), 0).astype(F32)
        for kind, out in ((0, key_out), (1, value_out)):
            total = jnp.zeros((NT, HD), F32)
            for i in range(ndp):
                block = sums[i, kind]
                for s in range(SEQS):
                    total = total + jnp.where(tenant == block[SEQS + s:SEQS + s + 1, :], block[s:s + 1, :], 0.0)
            out[...] = total[:, :HD // 2]


def on_device(ndp, nten, tokens, queries, out_grad, key_weight, value_weight, key_scale, value_scale, segment_ids, tenant_ids):
    chips = nten // 2
    rows_all, depth = tokens.shape
    nb = rows_all // RB
    wide = key_weight.shape[1]
    anywhere = pl.BlockSpec(memory_space=pl.ANY)
    vmem = pl.BlockSpec(memory_space=pltpu.VMEM)
    smem = pl.BlockSpec(memory_space=pltpu.SMEM)
    sem = pltpu.SemaphoreType.DMA
    many = max(1, (chips - 1) * nb)
    low, sums = pl.pallas_call(
        functools.partial(inner, ndp, nten),
        out_shape=(
            jax.ShapeDtypeStruct((rows_all, 2 * wide), BF16),
            jax.ShapeDtypeStruct((ndp, 2, 2 * SEQS, HD), F32),
        ),
        in_specs=[anywhere] * 5 + [vmem] * 3 + [smem],
        out_specs=(vmem, vmem),
        scratch_shapes=[
            pltpu.VMEM(tokens.shape, BF16),
            pltpu.VMEM(queries.shape, BF16),
            pltpu.VMEM(out_grad.shape, BF16),
            pltpu.VMEM(key_weight.shape, BF16),
            pltpu.VMEM(value_weight.shape, BF16),
            pltpu.VMEM((2, chips, rows_all, HD), F32),
            pltpu.VMEM((chips, rows_all, HD), F32),
            pltpu.VMEM((max(1, chips - 1), rows_all, HD), F32),
            pltpu.VMEM((rows_all, HD), F32),
            pltpu.VMEM((2, rows_all, HD), BF16),
            pltpu.VMEM((rows_all, HD), F32),
            pltpu.VMEM((LONGEST + RB, RB), F32),
            pltpu.VMEM((2, rows_all, HD), F32),
            pltpu.VMEM((rows_all, HD), F32),
            pltpu.VMEM((2, chips, rows_all, HD), BF16),
            pltpu.VMEM((ndp, 2, 2 * SEQS, HD), F32),
            sem((2 * KC,)), sem((2 * KC,)), sem((nb,)), sem((nb,)),
            sem((nb,)), sem((nb,)), sem((many,)), sem((many,)), sem((nb,)), sem((nb,)), sem((nb,)), sem((nb,)),
            sem((nb,)), sem((nb,)), sem((many,)), sem((many,)), sem((many,)), sem((many,)),
            sem((2 * ndp,)), sem((2 * ndp,)),
        ],
        compiler_params=pltpu.CompilerParams(
            collective_id=0, has_side_effects=True, vmem_limit_bytes=VMEM_LIMIT),
    )(tokens, queries, out_grad, key_weight, value_weight, key_scale, value_scale, segment_ids, tenant_ids)

    block = min(512, depth)
    return pl.pallas_call(
        functools.partial(closing, ndp),
        grid=(depth // block,),
        out_shape=(
            jax.ShapeDtypeStruct((rows_all, depth), BF16),
            jax.ShapeDtypeStruct((NT, HD // 2), F32),
            jax.ShapeDtypeStruct((NT, HD // 2), F32),
        ),
        in_specs=[
            pl.BlockSpec((rows_all, 2 * wide), lambda i: (0, 0)),
            pl.BlockSpec((block, wide), lambda i: (i, 0)),
            pl.BlockSpec((block, wide), lambda i: (i, 0)),
            pl.BlockSpec((ndp, 2, 2 * SEQS, HD), lambda i: (0, 0, 0, 0)),
        ],
        out_specs=(
            pl.BlockSpec((rows_all, block), lambda i: (0, i)),
            pl.BlockSpec((NT, HD // 2), lambda i: (0, 0)),
            pl.BlockSpec((NT, HD // 2), lambda i: (0, 0)),
        ),
        compiler_params=pltpu.CompilerParams(vmem_limit_bytes=VMEM_LIMIT),
    )(low, key_weight, value_weight, sums)


def solution(mesh):
    return jax.shard_map(
        functools.partial(on_device, mesh.shape["dp"], mesh.shape["tensor"]),
        mesh=mesh,
        in_specs=(
            P("dp", "tensor"),
            P("dp", "tensor"),
            P("dp", "tensor"),
            P("tensor", None),
            P("tensor", None),
            P(),
            P(),
            P("dp", None),
            P("dp", None),
        ),
        out_specs=(P("dp", "tensor"), P(None, "tensor"), P(None, "tensor")),
        check_vma=False,
    )
```

time: 221 us -> 45 us (0.20)
  matrix products: 63.1 us -> 0 us
  waiting for transfers between devices: 59.7 us -> 0 us
  blocking collectives: 37.7 us -> 0 us
  Pallas kernels: 0 us -> 37 us
  local copies, waits for them, and re-layouts: 31.1 us -> 6.89 us
  between operations: 14 us -> 0.67 us
  other arithmetic: 13 us -> 0 us
    dot_general x40 -> x0, matrix products: 63.1 us -> none  [the longest x8 18.7 us: head_grads(): lax.dot_general(score_grad, query_head, (((0,), (0,)), ((), ())), preferr...]
    reduce_scatter x2 -> x0, waiting for transfers between devices: 42.5 us -> none  [the longest x1 23.9 us: on_device(): lax.psum_scatter(key_partial_sum, 'tensor', scatter_dimension=1, tiled=True)]
    psum x1 -> x0, blocking collectives: 37.7 us -> none  [on_device(): key_total, value_total = lax.psum((key_tenant, value_tenant), 'dp')]
    pallas_call x0 -> x2, Pallas kernels: none -> 37 us  [the longest x1 31.3 us: on_device(): pl.pallas_call(functools.partial(inner, ndp, nten), out_shape=(jax.ShapeD...]
    all_gather x1 -> x0, waiting for transfers between devices: 17.2 us -> none  [on_device(): lax.all_gather(partials.astype(jnp.bfloat16), 'tensor', axis=1, tiled=True)]
    dynamic_slice x16 -> x0, local copies, waits for them, and re-layouts: 13.5 us -> none  [one_head(): out_head = lax.dynamic_slice_in_dim(out_grad, column, head_width, 1)]
    while x48 -> x0, local copies, waits for them, and re-layouts: 6.36 us -> none
    reduce_sum x10 -> x0, other arithmetic: 5.54 us -> none  [the longest x1 3.87 us: on_device(): summed = jnp.sum(shaped, axis=2)]
  transfers between devices with their start and end apart: 5 -> 0, of which waited for: 3 -> 0; matrix products, arithmetic and copies ran while one was open for 4% -> 0% of each run, Pallas kernels for 0% -> 0%
where the time goes in v1:
time: 45 us; the launch traced here: 44.5 us
  Pallas kernels  37 us (82%)
  local copies, waits for them, and re-layouts  6.89 us (15%)
  between operations  0.67 us (1%)
    pallas_call x1, Pallas kernels, on_device(): pl.pallas_call(functools.partial(inner, ndp, nten), out_shape=(jax.ShapeD...  31.3 us
    unnamed x18, local copies, waits for them, and re-layouts  6.89 us
    pallas_call x1, Pallas kernels, on_device(): pl.pallas_call(functools.partial(closing, ndp), grid=(depth // block,), o...  5.7 us

profile of v1, /device:TPU:0, one launch (start us, length us, event | category | flops | bytes accessed | tf_op | source)
XLA Modules:
  0.0 44.5 jit_solution(11360062716661402950)
XLA Ops:
  0.6 0.0 copy-start
  0.6 1.6 %copy-done = bf16[4096,256]{1,0:T(8,128)(2,1)S(1)} copy-done((bf16[4096,256]{1,0:T(8,128)(2,1)S(1)}, bf16[4096,256]{1,0:T(8,128)(2,1)}, u32[]{:S(2)}) %copy-start) | copy-done | bytes 2097176
  2.2 0.0 copy-start.3
  2.2 1.2 %copy-done.3 = bf16[512,1024]{1,0:T(8,128)(2,1)S(1)} copy-done((bf16[512,1024]{1,0:T(8,128)(2,1)S(1)}, bf16[512,1024]{1,0:T(8,128)(2,1)}, u32[]{:S(2)}) %copy-start.3) | copy-done | bytes 1048600
  3.5 0.0 copy-start.4
  3.5 1.2 %copy-done.4 = bf16[512,1024]{1,0:T(8,128)(2,1)S(1)} copy-done((bf16[512,1024]{1,0:T(8,128)(2,1)S(1)}, bf16[512,1024]{1,0:T(8,128)(2,1)}, u32[]{:S(2)}) %copy-start.4) | copy-done | bytes 1048600
  4.7 0.0 copy-start.5
  4.7 0.8 %copy-done.5 = f32[32,256]{1,0:T(8,128)S(1)} copy-done((f32[32,256]{1,0:T(8,128)S(1)}, f32[32,256]{1,0:T(8,128)}, u32[]{:S(2)}) %copy-start.5) | copy-done | bytes 32792
  5.4 0.0 copy-start.6
  5.4 0.8 %copy-done.6 = f32[32,256]{1,0:T(8,128)S(1)} copy-done((f32[32,256]{1,0:T(8,128)S(1)}, f32[32,256]{1,0:T(8,128)}, u32[]{:S(2)}) %copy-start.6) | copy-done | bytes 32792
  6.2 0.0 copy-start.7
  6.2 0.7 %copy-done.7 = s32[1,512]{1,0:T(1,128)S(1)} copy-done((s32[1,512]{1,0:T(1,128)S(1)}, s32[1,512]{1,0:T(1,128)}, u32[]{:S(2)}) %copy-start.7) | copy-done | bytes 2072
  6.9 0.0 copy-start.8
  6.9 0.7 %copy-done.8 = s32[1,4]{1,0:T(1,128)S(1)} copy-done((s32[1,4]{1,0:T(1,128)S(1)}, s32[1,4]{1,0:T(1,128)}, u32[]{:S(2)}) %copy-start.8) | copy-done | bytes 40
  7.5 0.0 copy-start.1
  7.5 0.0 copy-start.2
  7.5 31.3 %shard_map.112 = (bf16[512,512]{1,0:T(8,128)(2,1)S(1)}, f32[8,2,8,128]{3,2,1,0:T(8,128)S(1)}) custom-call(bf16[512,4096]{1,0:T(8,128)(2,1)} %tok_hbm.1, bf16[512,1024]{1,0:T(8,128)(2,1)S(1)} %copy-done.3, bf16[512,1024]{1,0:T(8,128)(2,1)S(1)} %copy-done.4, bf16[4096,256]{1,0:T(8,128)(2,1)S(1)} %copy-done, bf16[4096,256]{1,0:T(8,128)(2,1)} %vw.1, ...), custom_call_target="tpu_custom_call" | custom-call | tf_op jit(solution)/shard_map/pallas_call | solution.py:325
  38.8 0.0 copy-done.1
  38.8 0.0 copy-done.2
  38.8 5.7 %shard_map.113 = (bf16[512,4096]{1,0:T(8,128)(2,1)}, f32[32,64]{1,0:T(8,128)}, f32[32,64]{1,0:T(8,128)}) custom-call(bf16[512,512]{1,0:T(8,128)(2,1)S(1)} %get-tuple-element.5.low, bf16[4096,256]{1,0:T(8,128)(2,1)S(1)} %copy-done.1, bf16[4096,256]{1,0:T(8,128)(2,1)S(1)} %copy-done.2, f32[8,2,8,128]{3,2,1,0:T(8,128)S(1)} %get-tuple-element.6.sums), custom_call_target="tpu_custom_call" | custom-call | tf_op jit(solution)/shard_map/pallas_call | solution.py:360
Async XLA Ops:
  0.6 1.6 %copy-start = (bf16[4096,256]{1,0:T(8,128)(2,1)S(1)}, bf16[4096,256]{1,0:T(8,128)(2,1)}, u32[]{:S(2)}) copy-start(bf16[4096,256]{1,0:T(8,128)(2,1)} %kw.1) | copy-start | bytes 6291460
  2.2 1.2 %copy-start.3 = (bf16[512,1024]{1,0:T(8,128)(2,1)S(1)}, bf16[512,1024]{1,0:T(8,128)(2,1)}, u32[]{:S(2)}) copy-start(bf16[512,1024]{1,0:T(8,128)(2,1)} %q_hbm.1) | copy-start | bytes 3145732
  3.5 1.2 %copy-start.4 = (bf16[512,1024]{1,0:T(8,128)(2,1)S(1)}, bf16[512,1024]{1,0:T(8,128)(2,1)}, u32[]{:S(2)}) copy-start(bf16[512,1024]{1,0:T(8,128)(2,1)} %o_hbm.1) | copy-start | bytes 3145732
  4.7 0.8 %copy-start.5 = (f32[32,256]{1,0:T(8,128)S(1)}, f32[32,256]{1,0:T(8,128)}, u32[]{:S(2)}) copy-start(f32[32,256]{1,0:T(8,128)} %ks.1) | copy-start | bytes 98308
  5.4 0.8 %copy-start.6 = (f32[32,256]{1,0:T(8,128)S(1)}, f32[32,256]{1,0:T(8,128)}, u32[]{:S(2)}) copy-start(f32[32,256]{1,0:T(8,128)} %vs.1) | copy-start | bytes 98308
  6.2 0.7 %copy-start.7 = (s32[1,512]{1,0:T(1,128)S(1)}, s32[1,512]{1,0:T(1,128)}, u32[]{:S(2)}) copy-start(s32[1,512]{1,0:T(1,128)} %seg.1) | copy-start | bytes 6148
  6.9 0.7 %copy-start.8 = (s32[1,4]{1,0:T(1,128)S(1)}, s32[1,4]{1,0:T(1,128)}, u32[]{:S(2)}) copy-start(s32[1,4]{1,0:T(1,128)} %tenants.1) | copy-start | bytes 52
  7.5 31.3 %copy-start.1 = (bf16[4096,256]{1,0:T(8,128)(2,1)S(1)}, bf16[4096,256]{1,0:T(8,128)(2,1)}, u32[]{:S(2)}) copy-start(bf16[4096,256]{1,0:T(8,128)(2,1)} %kw.1) | copy-start | bytes 6291460
  7.5 31.3 %copy-start.2 = (bf16[4096,256]{1,0:T(8,128)(2,1)S(1)}, bf16[4096,256]{1,0:T(8,128)(2,1)}, u32[]{:S(2)}) copy-start(bf16[4096,256]{1,0:T(8,128)(2,1)} %vw.1) | copy-start | bytes 6291460

commit v2 on v1

--- a/solution.py
+++ b/solution.py
@@ -16,7 +16,8 @@
 HD = 128
 RB = 128
 LONGEST = 256
-VMEM_LIMIT = 48 * 1024 * 1024
+VMEM_LIMIT = 64 * 1024 * 1024
+TOGETHER = 4
 KC = 4
 
 
@@ -29,10 +30,11 @@
 
 
 def inner(
-    ndp, nten, tok_hbm, q_hbm, o_hbm, kw_hbm, vw_hbm, ks, vs, seg, tenants,
+    ndp, nten, tok_hbm, q_hbm, o_hbm, kw_hbm, vw_hbm, ks_hbm, vs_hbm, seg_hbm, tenants_hbm,
     low_out, sums_out,
     tok, q, o, kw, vw, part, from_core, from_chip, base, kv, factor, bias, grads, grads_in, lows, sums,
-    sem_w, sem_t, sem_q, sem_o,
+    ks, vs, seg, tenants,
+    sem_w, sem_t, sem_q, sem_o, sem_p,
     s1, r1, s2, r2, s3, r3, s4, r4, s5, r5, s6, r6, s7, r7, sg, rg,
 ):
     chips = nten // 2
@@ -66,6 +68,11 @@
     for b in range(nb):
         loads["q", b] = pltpu.make_async_copy(q_hbm.at[rows(b)], q.at[rows(b)], sem_q.at[b])
         loads["o", b] = pltpu.make_async_copy(o_hbm.at[rows(b)], o.at[rows(b)], sem_o.at[b])
+    small = [
+        pltpu.make_async_copy(src, dst, sem_p.at[i])
+        for i, (src, dst) in enumerate(((ks_hbm, ks), (vs_hbm, vs), (seg_hbm, seg), (tenants_hbm, tenants)))]
+    for copy in small:
+        copy.start()
     for k in range(KC):
         loads["k", k].start()
         loads["v", k].start()
@@ -99,6 +106,8 @@
 
     sent = []
 
+    for copy in small:
+        copy.wait()
     segments = seg[...]
     counts = [jnp.sum(jnp.where(segments == s, 1.0, 0.0), axis=1, keepdims=True) for s in range(SEQS)]
     bounds = [jnp.zeros((1, 1), F32)]
@@ -185,13 +194,12 @@
         width = (b + 1 - first) * RB
         keys_at = pl.ds(first * RB, width)
 
-        def pair(i, _):
-            c0 = pl.multiple_of(i * 2 * HD, 2 * HD)
-            c1 = pl.multiple_of(i * 2 * HD + HD, HD)
-            qh = jnp.concatenate([q[rows(b), pl.ds(c0, HD)], q[rows(b), pl.ds(c1, HD)]], axis=0)
-            oh = jnp.concatenate([o[rows(b), pl.ds(c0, HD)], o[rows(b), pl.ds(c1, HD)]], axis=0)
+        def several(i, _):
+            cols = [pl.ds(pl.multiple_of((i * TOGETHER + n) * HD, HD), HD) for n in range(TOGETHER)]
+            qh = jnp.concatenate([q[rows(b), col] for col in cols], axis=0)
+            oh = jnp.concatenate([o[rows(b), col] for col in cols], axis=0)
             hidden = bias[pl.ds(0, width), :]
-            scores = dot_nt(kv[0, keys_at, :], qh) + jnp.concatenate([hidden, hidden], axis=1)
+            scores = dot_nt(kv[0, keys_at, :], qh) + jnp.concatenate([hidden] * TOGETHER, axis=1)
             grad = dot_nt(kv[1, keys_at, :], oh)
             peak = jnp.max(scores, axis=0, keepdims=True)
             e = jnp.exp2((scores - peak) * to_exp2)
@@ -203,7 +211,7 @@
             grads[0, keys_at, :] = grads[0, keys_at, :] + dot_nn(score_grad, qh)
             return 0
 
-        lax.fori_loop(lo, hi, pair, 0)
+        lax.fori_loop(lo, hi, several, 0)
 
     def grads_to_core(b):
         sent.append(send(grads.at[other, rows(b)], grads_in.at[rows(b)], s4.at[b], r4.at[b], partner))
@@ -242,7 +250,7 @@
         to_chips(b)
     finish(0)
     finish(1)
-    pairs = heads // 2
+    pairs = heads // TOGETHER
     for b in range(nb):
         ready(b)
         last = b == nb - 1
@@ -317,9 +325,8 @@
     rows_all, depth = tokens.shape
     nb = rows_all // RB
     wide = key_weight.shape[1]
-    anywhere = pl.BlockSpec(memory_space=pl.ANY)
+    hbm = pl.BlockSpec(memory_space=pltpu.HBM)
     vmem = pl.BlockSpec(memory_space=pltpu.VMEM)
-    smem = pl.BlockSpec(memory_space=pltpu.SMEM)
     sem = pltpu.SemaphoreType.DMA
     many = max(1, (chips - 1) * nb)
     low, sums = pl.pallas_call(
@@ -328,7 +335,7 @@
             jax.ShapeDtypeStruct((rows_all, 2 * wide), BF16),
             jax.ShapeDtypeStruct((ndp, 2, 2 * SEQS, HD), F32),
         ),
-        in_specs=[anywhere] * 5 + [vmem] * 3 + [smem],
+        in_specs=[hbm] * 9,
         out_specs=(vmem, vmem),
         scratch_shapes=[
             pltpu.VMEM(tokens.shape, BF16),
@@ -347,7 +354,11 @@
             pltpu.VMEM((rows_all, HD), F32),
             pltpu.VMEM((2, chips, rows_all, HD), BF16),
             pltpu.VMEM((ndp, 2, 2 * SEQS, HD), F32),
-            sem((2 * KC,)), sem((2 * KC,)), sem((nb,)), sem((nb,)),
+            pltpu.VMEM(key_scale.shape, F32),
+            pltpu.VMEM(value_scale.shape, F32),
+            pltpu.VMEM(segment_ids.shape, jnp.int32),
+            pltpu.SMEM(tenant_ids.shape, jnp.int32),
+            sem((2 * KC,)), sem((2 * KC,)), sem((nb,)), sem((nb,)), sem((4,)),
             sem((nb,)), sem((nb,)), sem((many,)), sem((many,)), sem((nb,)), sem((nb,)), sem((nb,)), sem((nb,)),
             sem((nb,)), sem((nb,)), sem((many,)), sem((many,)), sem((many,)), sem((many,)),
             sem((2 * ndp,)), sem((2 * ndp,)),
@@ -356,7 +367,7 @@
             collective_id=0, has_side_effects=True, vmem_limit_bytes=VMEM_LIMIT),
     )(tokens, queries, out_grad, key_weight, value_weight, key_scale, value_scale, segment_ids, tenant_ids)
 
-    block = min(512, depth)
+    block = min(1024, depth)
     return pl.pallas_call(
         functools.partial(closing, ndp),
         grid=(depth // block,),

time: 45 us -> 36.1 us (0.80)
  local copies, waits for them, and re-layouts: 6.89 us -> 0 us
  Pallas kernels: 37 us -> 35.2 us
    unnamed x18 -> x0, local copies, waits for them, and re-layouts: 6.89 us -> none
    pallas_call x1, Pallas kernels: 31.3 us -> 28.9 us  [on_device(): pl.pallas_call(functools.partial(inner, ndp, nten), out_shape=(jax.ShapeD...]
    pallas_call x1, Pallas kernels: 5.7 us -> 6.38 us  [on_device(): pl.pallas_call(functools.partial(closing, ndp), grid=(depth // block,), o...]
where the time goes in v2:
time: 36.1 us; the launch traced here: 35.9 us
  Pallas kernels  35.2 us (98%)
  between operations  0.64 us (2%)
    pallas_call x1, Pallas kernels, on_device(): pl.pallas_call(functools.partial(inner, ndp, nten), out_shape=(jax.ShapeD...  28.9 us
    pallas_call x1, Pallas kernels, on_device(): pl.pallas_call(functools.partial(closing, ndp), grid=(depth // block,), o...  6.38 us

profile of v2, /device:TPU:0, one launch (start us, length us, event | category | flops | bytes accessed | tf_op | source)
XLA Modules:
  0.0 35.9 jit_solution(17887689998753608974)
XLA Ops:
  0.6 28.9 %shard_map.112 = (bf16[512,512]{1,0:T(8,128)(2,1)}, f32[8,2,8,128]{3,2,1,0:T(8,128)}) custom-call(bf16[512,4096]{1,0:T(8,128)(2,1)} %tok_hbm.1, bf16[512,1024]{1,0:T(8,128)(2,1)} %q_hbm.1, bf16[512,1024]{1,0:T(8,128)(2,1)} %o_hbm.1, bf16[4096,256]{1,0:T(8,128)(2,1)} %kw.1, bf16[4096,256]{1,0:T(8,128)(2,1)} %vw.1, f32[32,256]{1,0:T(8,128)} %ks_hbm.1, ...), custom_call_target="tpu_custom_call" | custom-call | tf_op jit(solution)/shard_map/pallas_call | solution.py:332
  29.5 6.4 %shard_map.113 = (bf16[512,4096]{1,0:T(8,128)(2,1)}, f32[32,64]{1,0:T(8,128)}, f32[32,64]{1,0:T(8,128)}) custom-call(bf16[512,512]{1,0:T(8,128)(2,1)} %get-tuple-element.5.low, bf16[4096,256]{1,0:T(8,128)(2,1)} %kw.1, bf16[4096,256]{1,0:T(8,128)(2,1)} %vw.1, f32[8,2,8,128]{3,2,1,0:T(8,128)} %get-tuple-element.6.sums), custom_call_target="tpu_custom_call" | custom-call | tf_op jit(solution)/shard_map/pallas_call | solution.py:371

commit v3 on v2

--- a/solution.py
+++ b/solution.py
@@ -56,15 +56,10 @@
     def rows(b):
         return pl.ds(b * RB, RB)
 
+    def load(src, dst, at, cols, sem):
+        return pltpu.make_async_copy(src.at[at, cols], dst.at[at, cols], sem)
+
     loads = {}
-    for k in range(KC):
-        ks_ = pl.ds(k * kc, kc)
-        loads["k", k] = pltpu.make_async_copy(kw_hbm.at[ks_], kw.at[ks_], sem_w.at[k])
-        loads["v", k] = pltpu.make_async_copy(vw_hbm.at[ks_], vw.at[ks_], sem_w.at[KC + k])
-        loads["t", 0, k] = pltpu.make_async_copy(
-            tok_hbm.at[pl.ds(0, half), ks_], tok.at[pl.ds(0, half), ks_], sem_t.at[k])
-        loads["t", 1, k] = pltpu.make_async_copy(
-            tok_hbm.at[pl.ds(half, half), ks_], tok.at[pl.ds(half, half), ks_], sem_t.at[KC + k])
     for b in range(nb):
         loads["q", b] = pltpu.make_async_copy(q_hbm.at[rows(b)], q.at[rows(b)], sem_q.at[b])
         loads["o", b] = pltpu.make_async_copy(o_hbm.at[rows(b)], o.at[rows(b)], sem_o.at[b])
@@ -74,11 +69,12 @@
     for copy in small:
         copy.start()
     for k in range(KC):
-        loads["k", k].start()
-        loads["v", k].start()
-        loads["t", 0, k].start()
+        kk = pl.ds(k * kc, kc)
+        load(kw_hbm, kw, kk, slice(None), sem_w.at[k]).start()
+        load(vw_hbm, vw, kk, slice(None), sem_w.at[KC + k]).start()
+        load(tok_hbm, tok, pl.ds(0, half), kk, sem_t.at[k]).start()
     for k in range(KC):
-        loads["t", 1, k].start()
+        load(tok_hbm, tok, pl.ds(half, half), pl.ds(k * kc, kc), sem_t.at[KC + k]).start()
     for b in range(nb):
         loads["q", b].start()
         loads["o", b].start()
@@ -136,22 +132,30 @@
 
     pl.semaphore_wait(barrier, count)
 
-    def project(r):
+    def project(r, lo, hi):
         rr = pl.ds(r * half, half)
-        for k in range(KC):
-            kk = pl.ds(k * kc, kc)
+
+        def step(k, first):
+            kk = pl.ds(pl.multiple_of(k * kc, kc), kc)
             if r == 0:
-                loads["k", k].wait()
-                loads["v", k].wait()
-            loads["t", r, k].wait()
+                load(kw_hbm, kw, kk, slice(None), sem_w.at[k]).wait()
+                load(vw_hbm, vw, kk, slice(None), sem_w.at[KC + k]).wait()
+            load(tok_hbm, tok, rr, kk, sem_t.at[r * KC + k]).wait()
             block = tok[rr, kk]
             for kind, weight in ((0, kw), (1, vw)):
                 value = dot_nn(block, weight[kk, :])
                 for h in range(chips):
                     piece = value[:, h * HD:(h + 1) * HD]
-                    if k:
-                        piece = piece + part[kind, h, rr, :]
-                    part[kind, h, rr, :] = piece
+                    part[kind, h, rr, :] = piece if first else piece + part[kind, h, rr, :]
+
+        if lo == 0:
+            step(0, True)
+
+        def more(k, _):
+            step(k, False)
+            return 0
+
+        lax.fori_loop(max(lo, 1), hi, more, 0)
 
     def to_core(b):
         sent.append(send(part.at[other, :, rows(b)], from_core.at[:, rows(b)], s1.at[b], r1.at[b], partner))
@@ -196,19 +200,25 @@
 
         def several(i, _):
             cols = [pl.ds(pl.multiple_of((i * TOGETHER + n) * HD, HD), HD) for n in range(TOGETHER)]
-            qh = jnp.concatenate([q[rows(b), col] for col in cols], axis=0)
-            oh = jnp.concatenate([o[rows(b), col] for col in cols], axis=0)
-            hidden = bias[pl.ds(0, width), :]
-            scores = dot_nt(kv[0, keys_at, :], qh) + jnp.concatenate([hidden] * TOGETHER, axis=1)
-            grad = dot_nt(kv[1, keys_at, :], oh)
-            peak = jnp.max(scores, axis=0, keepdims=True)
-            e = jnp.exp2((scores - peak) * to_exp2)
-            probs = e * (1.0 / jnp.sum(e, axis=0, keepdims=True))
-            low = probs.astype(BF16)
-            delta = jnp.sum(low.astype(F32) * grad, axis=0, keepdims=True)
-            score_grad = (probs * (grad - delta)).astype(BF16)
-            grads[1, keys_at, :] = grads[1, keys_at, :] + dot_nn(low, oh)
-            grads[0, keys_at, :] = grads[0, keys_at, :] + dot_nn(score_grad, qh)
+            keys, values, hidden = kv[0, keys_at, :], kv[1, keys_at, :], bias[pl.ds(0, width), :]
+            qs, outs, lows_, score_grads = [], [], [], []
+            for col in cols:
+                qh, oh = q[rows(b), col], o[rows(b), col]
+                scores = dot_nt(keys, qh) + hidden
+                grad = dot_nt(values, oh)
+                peak = jnp.max(scores, axis=0, keepdims=True)
+                e = jnp.exp2((scores - peak) * to_exp2)
+                probs = e * (1.0 / jnp.sum(e, axis=0, keepdims=True))
+                low = probs.astype(BF16)
+                delta = jnp.sum(low.astype(F32) * grad, axis=0, keepdims=True)
+                qs.append(qh)
+                outs.append(oh)
+                lows_.append(low)
+                score_grads.append((probs * (grad - delta)).astype(BF16))
+            grads[1, keys_at, :] = grads[1, keys_at, :] + dot_nn(
+                jnp.concatenate(lows_, axis=1), jnp.concatenate(outs, axis=0))
+            grads[0, keys_at, :] = grads[0, keys_at, :] + dot_nn(
+                jnp.concatenate(score_grads, axis=1), jnp.concatenate(qs, axis=0))
             return 0
 
         lax.fori_loop(lo, hi, several, 0)
@@ -239,13 +249,15 @@
             arrived(lows.at[c, j, rows(b)], r6.at[i])
             sent.append(send(lows.at[c, j, rows(b)], lows.at[c, j, rows(b)], s7.at[i], r7.at[i], partner))
 
-    for r in range(2):
-        project(r)
-        for b in range(r * nb // 2, (r + 1) * nb // 2):
-            to_core(b)
-        if r == 0:
-            for b in range(nb // 2):
-                to_chips(b)
+    project(0, 0, KC)
+    for b in range(nb // 2):
+        to_core(b)
+    project(1, 0, KC // 2)
+    for b in range(nb // 2):
+        to_chips(b)
+    project(1, KC // 2, KC)
+    for b in range(nb // 2, nb):
+        to_core(b)
     for b in range(nb // 2, nb):
         to_chips(b)
     finish(0)
@@ -304,9 +316,8 @@
 
 
 def closing(ndp, low, kw, vw, sums, grad_out, key_out, value_out):
-    wide = kw.shape[1]
-    grad = dot_nt(low[:, :wide], kw[...]) + dot_nt(low[:, wide:], vw[...])
-    grad_out[...] = grad.astype(BF16)
+    weights = jnp.concatenate([kw[...], vw[...]], axis=1)
+    grad_out[...] = dot_nt(low[...], weights).astype(BF16)
 
     @pl.when(pl.program_id(0) == 0)
     def _():
@@ -367,7 +378,7 @@
             collective_id=0, has_side_effects=True, vmem_limit_bytes=VMEM_LIMIT),
     )(tokens, queries, out_grad, key_weight, value_weight, key_scale, value_scale, segment_ids, tenant_ids)
 
-    block = min(1024, depth)
+    block = min(512, depth)
     return pl.pallas_call(
         functools.partial(closing, ndp),
         grid=(depth // block,),

time: 36.1 us -> 38.5 us (1.066)
  Pallas kernels: 35.2 us -> 37.6 us
    pallas_call x1, Pallas kernels: 6.38 us -> 8.42 us  [on_device(): pl.pallas_call(functools.partial(closing, ndp), grid=(depth // block,), o...]
where the time goes in v3:
time: 38.5 us; the launch traced here: 38.2 us
  Pallas kernels  37.6 us (98%)
  between operations  0.64 us (2%)
    pallas_call x1, Pallas kernels, on_device(): pl.pallas_call(functools.partial(inner, ndp, nten), out_shape=(jax.ShapeD...  29.2 us
    pallas_call x1, Pallas kernels, on_device(): pl.pallas_call(functools.partial(closing, ndp), grid=(depth // block,), o...  8.42 us

profile of v3, /device:TPU:0, one launch (start us, length us, event | category | flops | bytes accessed | tf_op | source)
XLA Modules:
  0.0 38.2 jit_solution(12738331873094089327)
XLA Ops:
  0.6 29.2 %shard_map.112 = (bf16[512,512]{1,0:T(8,128)(2,1)}, f32[8,2,8,128]{3,2,1,0:T(8,128)}) custom-call(bf16[512,4096]{1,0:T(8,128)(2,1)} %tok_hbm.1, bf16[512,1024]{1,0:T(8,128)(2,1)} %q_hbm.1, bf16[512,1024]{1,0:T(8,128)(2,1)} %o_hbm.1, bf16[4096,256]{1,0:T(8,128)(2,1)} %kw.1, bf16[4096,256]{1,0:T(8,128)(2,1)} %vw.1, f32[32,256]{1,0:T(8,128)} %ks_hbm.1, ...), custom_call_target="tpu_custom_call" | custom-call | tf_op jit(solution)/shard_map/pallas_call | solution.py:343
  29.8 8.4 %shard_map.113 = (bf16[512,4096]{1,0:T(8,128)(2,1)}, f32[32,64]{1,0:T(8,128)}, f32[32,64]{1,0:T(8,128)}) custom-call(bf16[512,512]{1,0:T(8,128)(2,1)} %get-tuple-element.5.low, bf16[4096,256]{1,0:T(8,128)(2,1)} %kw.1, bf16[4096,256]{1,0:T(8,128)(2,1)} %vw.1, f32[8,2,8,128]{3,2,1,0:T(8,128)} %get-tuple-element.6.sums), custom_call_target="tpu_custom_call" | custom-call | tf_op jit(solution)/shard_map/pallas_call | solution.py:382

commit v4 on v3

--- a/solution.py
+++ b/solution.py
@@ -18,6 +18,7 @@
 LONGEST = 256
 VMEM_LIMIT = 64 * 1024 * 1024
 TOGETHER = 4
+FB = 512
 KC = 4
 
 
@@ -34,7 +35,7 @@
     low_out, sums_out,
     tok, q, o, kw, vw, part, from_core, from_chip, base, kv, factor, bias, grads, grads_in, lows, sums,
     ks, vs, seg, tenants,
-    sem_w, sem_t, sem_q, sem_o, sem_p,
+    sem_w, sem_t, sem_q, sem_o, sem_p, sem_s,
     s1, r1, s2, r2, s3, r3, s4, r4, s5, r5, s6, r6, s7, r7, sg, rg,
 ):
     chips = nten // 2
@@ -102,36 +103,6 @@
 
     sent = []
 
-    for copy in small:
-        copy.wait()
-    segments = seg[...]
-    counts = [jnp.sum(jnp.where(segments == s, 1.0, 0.0), axis=1, keepdims=True) for s in range(SEQS)]
-    bounds = [jnp.zeros((1, 1), F32)]
-    for s in range(SEQS):
-        bounds.append(bounds[-1] + counts[s])
-    start = jnp.zeros(segments.shape, F32)
-    for s in range(1, SEQS):
-        start = jnp.where(segments == s, bounds[s], start)
-    own_cols = pl.ds(pl.multiple_of(x * HD, HD), HD)
-    own_scale = ks[:, own_cols] * (1.0 - cf) + vs[:, own_cols] * cf
-    tenant = lax.broadcasted_iota(jnp.int32, (NT, HD), 0)
-    scale_rows = [
-        jnp.sum(jnp.where(tenant == tenants[0, s], own_scale, 0.0), axis=0, keepdims=True) for s in range(SEQS)]
-
-    def position(b):
-        return lax.broadcasted_iota(jnp.int32, (RB, HD), 0).astype(F32) + float(b * RB)
-
-    for b in range(nb):
-        pos = position(b)
-        f = jnp.broadcast_to(scale_rows[SEQS - 1], (RB, HD))
-        for s in range(SEQS - 2, -1, -1):
-            f = jnp.where(pos < bounds[s + 1], scale_rows[s], f)
-        factor[rows(b), :] = f
-        grads[0, rows(b), :] = jnp.zeros((RB, HD), F32)
-        grads[1, rows(b), :] = jnp.zeros((RB, HD), F32)
-
-    pl.semaphore_wait(barrier, count)
-
     def project(r, lo, hi):
         rr = pl.ds(r * half, half)
 
@@ -167,6 +138,9 @@
             part[c, j, rows(b), :] = part[c, j, rows(b), :] + from_core[j, rows(b), :]
             i = (p - 1) * nb + b
             sent.append(send(part.at[c, j, rows(b)], from_chip.at[p - 1, rows(b)], s2.at[i], r2.at[i], peers[p - 1]))
+
+    def position(b):
+        return lax.broadcasted_iota(jnp.int32, (RB, HD), 0).astype(F32) + float(b * RB)
 
     def finish(b):
         total = part[c, x, rows(b), :] + from_core[x, rows(b), :]
@@ -250,8 +224,33 @@
             sent.append(send(lows.at[c, j, rows(b)], lows.at[c, j, rows(b)], s7.at[i], r7.at[i], partner))
 
     project(0, 0, KC)
+    pl.semaphore_wait(barrier, count)
     for b in range(nb // 2):
         to_core(b)
+    for copy in small:
+        copy.wait()
+    segments = seg[...]
+    counts = [jnp.sum(jnp.where(segments == s, 1.0, 0.0), axis=1, keepdims=True) for s in range(SEQS)]
+    bounds = [jnp.zeros((1, 1), F32)]
+    for s in range(SEQS):
+        bounds.append(bounds[-1] + counts[s])
+    start = jnp.zeros(segments.shape, F32)
+    for s in range(1, SEQS):
+        start = jnp.where(segments == s, bounds[s], start)
+    own_cols = pl.ds(pl.multiple_of(x * HD, HD), HD)
+    own_scale = ks[:, own_cols] * (1.0 - cf) + vs[:, own_cols] * cf
+    tenant = lax.broadcasted_iota(jnp.int32, (NT, HD), 0)
+    scale_rows = [
+        jnp.sum(jnp.where(tenant == tenants[0, s], own_scale, 0.0), axis=0, keepdims=True) for s in range(SEQS)]
+
+    for b in range(nb):
+        pos = position(b)
+        f = jnp.broadcast_to(scale_rows[SEQS - 1], (RB, HD))
+        for s in range(SEQS - 2, -1, -1):
+            f = jnp.where(pos < bounds[s + 1], scale_rows[s], f)
+        factor[rows(b), :] = f
+        grads[0, rows(b), :] = jnp.zeros((RB, HD), F32)
+        grads[1, rows(b), :] = jnp.zeros((RB, HD), F32)
     project(1, 0, KC // 2)
     for b in range(nb // 2):
         to_chips(b)
@@ -297,9 +296,12 @@
         for p in range(1, chips):
             j = lax.rem(x + chips - p, chips)
             arrived(lows.at[other, j, rows(b)], r7.at[(p - 1) * nb + b])
+    saves = []
     for kind in range(2):
         for h in range(chips):
-            low_out[:, pl.ds((kind * chips + h) * HD, HD)] = lows[kind, h]
+            n = kind * chips + h
+            saves.append(pltpu.make_async_copy(lows.at[kind, h], low_out.at[:, pl.ds(n * HD, HD)], sem_s.at[n]))
+            saves[-1].start()
     for i in range(ndp):
         if i == 0:
             arrived(sums.at[0, other], rg.at[other])
@@ -311,24 +313,60 @@
             value = sums[i, core]
             turned = jnp.concatenate([value[:, HD // 2:], value[:, :HD // 2]], axis=1)
             sums_out[i, core] = value * (1.0 - cf) + turned * cf
+    for copy in saves:
+        copy.wait()
     for copy in sent:
         copy.wait_send()
 
 
-def closing(ndp, low, kw, vw, sums, grad_out, key_out, value_out):
-    weights = jnp.concatenate([kw[...], vw[...]], axis=1)
-    grad_out[...] = dot_nt(low[...], weights).astype(BF16)
-
-    @pl.when(pl.program_id(0) == 0)
-    def _():
-        tenant = lax.broadcasted_iota(jnp.int32, (NT, HD), 0).astype(F32)
-        for kind, out in ((0, key_out), (1, value_out)):
-            total = jnp.zeros((NT, HD), F32)
-            for i in range(ndp):
-                block = sums[i, kind]
-                for s in range(SEQS):
-                    total = total + jnp.where(tenant == block[SEQS + s:SEQS + s + 1, :], block[s:s + 1, :], 0.0)
-            out[...] = total[:, :HD // 2]
+def closing(
+    ndp, low_hbm, kw_hbm, vw_hbm, sums, grad_hbm, key_out, value_out, low, kw, vw, grad, sem_l, sem_k, sem_v, sem_g
+):
+    depth = kw.shape[0]
+    block = min(FB, depth)
+    count = depth // block
+
+    def load_low():
+        return pltpu.make_async_copy(low_hbm, low, sem_l.at[0])
+
+    def at(i):
+        return pl.ds(pl.multiple_of(i * block, block), block)
+
+    def load_key(i):
+        return pltpu.make_async_copy(kw_hbm.at[at(i)], kw.at[at(i)], sem_k.at[i])
+
+    def load_value(i):
+        return pltpu.make_async_copy(vw_hbm.at[at(i)], vw.at[at(i)], sem_v.at[i])
+
+    def save(i):
+        return pltpu.make_async_copy(grad.at[:, at(i)], grad_hbm.at[:, at(i)], sem_g.at[i])
+
+    load_low().start()
+    for i in range(count):
+        load_key(i).start()
+        load_value(i).start()
+    load_low().wait()
+
+    def step(i, _):
+        load_key(i).wait()
+        load_value(i).wait()
+        weights = jnp.concatenate([kw[at(i), :], vw[at(i), :]], axis=1)
+        grad[:, at(i)] = dot_nt(low[...], weights).astype(BF16)
+        save(i).start()
+        return 0
+
+    lax.fori_loop(0, count, step, 0)
+
+    tenant = lax.broadcasted_iota(jnp.int32, (NT, HD), 0).astype(F32)
+    for kind, out in ((0, key_out), (1, value_out)):
+        total = jnp.zeros((NT, HD), F32)
+        for i in range(ndp):
+            rows = sums[i, kind]
+            for s in range(SEQS):
+                total = total + jnp.where(tenant == rows[SEQS + s:SEQS + s + 1, :], rows[s:s + 1, :], 0.0)
+        out[...] = total[:, :HD // 2]
+    for i in range(count):
+        save(i).wait()
 
 
 def on_device(ndp, nten, tokens, queries, out_grad, key_weight, value_weight, key_scale, value_scale, segment_ids, tenant_ids):
@@ -347,7 +385,7 @@
             jax.ShapeDtypeStruct((ndp, 2, 2 * SEQS, HD), F32),
         ),
         in_specs=[hbm] * 9,
-        out_specs=(vmem, vmem),
+        out_specs=(hbm, vmem),
         scratch_shapes=[
             pltpu.VMEM(tokens.shape, BF16),
             pltpu.VMEM(queries.shape, BF16),
@@ -369,7 +407,7 @@
             pltpu.VMEM(value_scale.shape, F32),
             pltpu.VMEM(segment_ids.shape, jnp.int32),
             pltpu.SMEM(tenant_ids.shape, jnp.int32),
-            sem((2 * KC,)), sem((2 * KC,)), sem((nb,)), sem((nb,)), sem((4,)),
+            sem((2 * KC,)), sem((2 * KC,)), sem((nb,)), sem((nb,)), sem((4,)), sem((2 * chips,)),
             sem((nb,)), sem((nb,)), sem((many,)), sem((many,)), sem((nb,)), sem((nb,)), sem((nb,)), sem((nb,)),
             sem((nb,)), sem((nb,)), sem((many,)), sem((many,)), sem((many,)), sem((many,)),
             sem((2 * ndp,)), sem((2 * ndp,)),
@@ -378,26 +416,23 @@
             collective_id=0, has_side_effects=True, vmem_limit_bytes=VMEM_LIMIT),
     )(tokens, queries, out_grad, key_weight, value_weight, key_scale, value_scale, segment_ids, tenant_ids)
 
-    block = min(512, depth)
+    count = depth // min(FB, depth)
     return pl.pallas_call(
         functools.partial(closing, ndp),
-        grid=(depth // block,),
         out_shape=(
             jax.ShapeDtypeStruct((rows_all, depth), BF16),
             jax.ShapeDtypeStruct((NT, HD // 2), F32),
             jax.ShapeDtypeStruct((NT, HD // 2), F32),
         ),
-        in_specs=[
-            pl.BlockSpec((rows_all, 2 * wide), lambda i: (0, 0)),
-            pl.BlockSpec((block, wide), lambda i: (i, 0)),
-            pl.BlockSpec((block, wide), lambda i: (i, 0)),
-            pl.BlockSpec((ndp, 2, 2 * SEQS, HD), lambda i: (0, 0, 0, 0)),
+        in_specs=[hbm] * 3 + [vmem],
+        out_specs=(hbm, vmem, vmem),
+        scratch_shapes=[
+            pltpu.VMEM((rows_all, 2 * wide), BF16),
+            pltpu.VMEM(key_weight.shape, BF16),
+            pltpu.VMEM(value_weight.shape, BF16),
+            pltpu.VMEM((rows_all, depth), BF16),
+            sem((1,)), sem((count,)), sem((count,)), sem((count,)),
         ],
-        out_specs=(
-            pl.BlockSpec((rows_all, block), lambda i: (0, i)),
-            pl.BlockSpec((NT, HD // 2), lambda i: (0, 0)),
-            pl.BlockSpec((NT, HD // 2), lambda i: (0, 0)),
-        ),
         compiler_params=pltpu.CompilerParams(vmem_limit_bytes=VMEM_LIMIT),
     )(low, key_weight, value_weight, sums)
 

time: 38.5 us -> 37.7 us (0.979)
  Pallas kernels: 37.6 us -> 36.9 us
    pallas_call x1, Pallas kernels: 29.2 us -> 28.5 us  [on_device(): pl.pallas_call(functools.partial(inner, ndp, nten), out_shape=(jax.ShapeD...]
where the time goes in v4:
time: 37.7 us; the launch traced here: 37.5 us
  Pallas kernels  36.9 us (98%)
  between operations  0.64 us (2%)
    pallas_call x1, Pallas kernels, on_device(): pl.pallas_call(functools.partial(inner, ndp, nten), out_shape=(jax.ShapeD...  28.5 us
    pallas_call x1, Pallas kernels, on_device(): pl.pallas_call(functools.partial(closing, ndp), out_shape=(jax.ShapeDtype...  8.39 us

profile of v4, /device:TPU:0, one launch (start us, length us, event | category | flops | bytes accessed | tf_op | source)
XLA Modules:
  0.0 37.5 jit_solution(14816957936870697745)
XLA Ops:
  0.6 28.5 %shard_map.112 = (bf16[512,512]{1,0:T(8,128)(2,1)}, f32[8,2,8,128]{3,2,1,0:T(8,128)}) custom-call(bf16[512,4096]{1,0:T(8,128)(2,1)} %tok_hbm.1, bf16[512,1024]{1,0:T(8,128)(2,1)} %q_hbm.1, bf16[512,1024]{1,0:T(8,128)(2,1)} %o_hbm.1, bf16[4096,256]{1,0:T(8,128)(2,1)} %kw_hbm.3, bf16[4096,256]{1,0:T(8,128)(2,1)} %vw_hbm.3, f32[32,256]{1,0:T(8,128)} %ks_hbm.1, ...), custom_call_target="tpu_custom_call" | custom-call | tf_op jit(solution)/shard_map/pallas_call | solution.py:381
  29.2 8.4 %shard_map.113 = (bf16[512,4096]{1,0:T(8,128)(2,1)}, f32[32,64]{1,0:T(8,128)}, f32[32,64]{1,0:T(8,128)}) custom-call(bf16[512,512]{1,0:T(8,128)(2,1)} %get-tuple-element.5.low_hbm, bf16[4096,256]{1,0:T(8,128)(2,1)} %kw_hbm.3, bf16[4096,256]{1,0:T(8,128)(2,1)} %vw_hbm.3, f32[8,2,8,128]{3,2,1,0:T(8,128)} %get-tuple-element.6.sums), custom_call_target="tpu_custom_call" | custom-call | tf_op jit(solution)/shard_map/pallas_call | solution.py:420

commit v5 on v4

--- a/solution.py
+++ b/solution.py
@@ -19,7 +19,7 @@
 VMEM_LIMIT = 64 * 1024 * 1024
 TOGETHER = 4
 FB = 512
-KC = 4
+KD = 512
 
 
 def dot_nt(a, b):
@@ -42,8 +42,8 @@
     rows_all, depth = tok.shape
     nb = rows_all // RB
     look = LONGEST // RB
-    half = rows_all // 2
-    kc = depth // KC
+    kc = min(KD, depth)
+    pieces = depth // kc
     d = lax.axis_index("dp")
     t = lax.axis_index("tensor")
     x = t // 2
@@ -69,13 +69,11 @@
         for i, (src, dst) in enumerate(((ks_hbm, ks), (vs_hbm, vs), (seg_hbm, seg), (tenants_hbm, tenants)))]
     for copy in small:
         copy.start()
-    for k in range(KC):
+    for k in range(pieces):
         kk = pl.ds(k * kc, kc)
         load(kw_hbm, kw, kk, slice(None), sem_w.at[k]).start()
-        load(vw_hbm, vw, kk, slice(None), sem_w.at[KC + k]).start()
-        load(tok_hbm, tok, pl.ds(0, half), kk, sem_t.at[k]).start()
-    for k in range(KC):
-        load(tok_hbm, tok, pl.ds(half, half), pl.ds(k * kc, kc), sem_t.at[KC + k]).start()
+        load(vw_hbm, vw, kk, slice(None), sem_w.at[pieces + k]).start()
+        load(tok_hbm, tok, slice(None), kk, sem_t.at[k]).start()
     for b in range(nb):
         loads["q", b].start()
         loads["o", b].start()
@@ -103,30 +101,33 @@
 
     sent = []
 
-    def project(r, lo, hi):
-        rr = pl.ds(r * half, half)
+    def project():
+        deep = kc // 2
 
         def step(k, first):
             kk = pl.ds(pl.multiple_of(k * kc, kc), kc)
-            if r == 0:
-                load(kw_hbm, kw, kk, slice(None), sem_w.at[k]).wait()
-                load(vw_hbm, vw, kk, slice(None), sem_w.at[KC + k]).wait()
-            load(tok_hbm, tok, rr, kk, sem_t.at[r * KC + k]).wait()
-            block = tok[rr, kk]
-            for kind, weight in ((0, kw), (1, vw)):
-                value = dot_nn(block, weight[kk, :])
+            load(kw_hbm, kw, kk, slice(None), sem_w.at[k]).wait()
+            load(vw_hbm, vw, kk, slice(None), sem_w.at[pieces + k]).wait()
+            load(tok_hbm, tok, slice(None), kk, sem_t.at[k]).wait()
+            value = None
+            for n in range(2):
+                at = pl.ds(pl.multiple_of(k * kc + n * deep, deep), deep)
+                weights = jnp.concatenate([kw[at, :], vw[at, :]], axis=1)
+                term = dot_nn(tok[:, at], weights)
+                value = term if value is None else value + term
+            for kind in range(2):
                 for h in range(chips):
-                    piece = value[:, h * HD:(h + 1) * HD]
-                    part[kind, h, rr, :] = piece if first else piece + part[kind, h, rr, :]
-
-        if lo == 0:
-            step(0, True)
+                    n = kind * chips + h
+                    piece = value[:, n * HD:(n + 1) * HD]
+                    part[kind, h] = piece if first else piece + part[kind, h]
+
+        step(0, True)
 
         def more(k, _):
             step(k, False)
             return 0
 
-        lax.fori_loop(max(lo, 1), hi, more, 0)
+        lax.fori_loop(1, pieces, more, 0)
 
     def to_core(b):
         sent.append(send(part.at[other, :, rows(b)], from_core.at[:, rows(b)], s1.at[b], r1.at[b], partner))
@@ -223,9 +224,9 @@
             arrived(lows.at[c, j, rows(b)], r6.at[i])
             sent.append(send(lows.at[c, j, rows(b)], lows.at[c, j, rows(b)], s7.at[i], r7.at[i], partner))
 
-    project(0, 0, KC)
+    project()
     pl.semaphore_wait(barrier, count)
-    for b in range(nb // 2):
+    for b in range(nb):
         to_core(b)
     for copy in small:
         copy.wait()
@@ -251,13 +252,7 @@
         factor[rows(b), :] = f
         grads[0, rows(b), :] = jnp.zeros((RB, HD), F32)
         grads[1, rows(b), :] = jnp.zeros((RB, HD), F32)
-    project(1, 0, KC // 2)
-    for b in range(nb // 2):
-        to_chips(b)
-    project(1, KC // 2, KC)
-    for b in range(nb // 2, nb):
-        to_core(b)
-    for b in range(nb // 2, nb):
+    for b in range(nb):
         to_chips(b)
     finish(0)
     finish(1)
@@ -350,8 +345,9 @@
     def step(i, _):
         load_key(i).wait()
         load_value(i).wait()
-        weights = jnp.concatenate([kw[at(i), :], vw[at(i), :]], axis=1)
-        grad[:, at(i)] = dot_nt(low[...], weights).astype(BF16)
+        wide = kw.shape[1]
+        value = dot_nt(low[:, :wide], kw[at(i), :]) + dot_nt(low[:, wide:], vw[at(i), :])
+        grad[:, at(i)] = value.astype(BF16)
         save(i).start()
         return 0
 
@@ -377,6 +373,7 @@
     hbm = pl.BlockSpec(memory_space=pltpu.HBM)
     vmem = pl.BlockSpec(memory_space=pltpu.VMEM)
     sem = pltpu.SemaphoreType.DMA
+    pieces = depth // min(KD, depth)
     many = max(1, (chips - 1) * nb)
     low, sums = pl.pallas_call(
         functools.partial(inner, ndp, nten),
@@ -407,7 +404,7 @@
             pltpu.VMEM(value_scale.shape, F32),
             pltpu.VMEM(segment_ids.shape, jnp.int32),
             pltpu.SMEM(tenant_ids.shape, jnp.int32),
-            sem((2 * KC,)), sem((2 * KC,)), sem((nb,)), sem((nb,)), sem((4,)), sem((2 * chips,)),
+            sem((2 * pieces,)), sem((pieces,)), sem((nb,)), sem((nb,)), sem((4,)), sem((2 * chips,)),
             sem((nb,)), sem((nb,)), sem((many,)), sem((many,)), sem((nb,)), sem((nb,)), sem((nb,)), sem((nb,)),
             sem((nb,)), sem((nb,)), sem((many,)), sem((many,)), sem((many,)), sem((many,)),
             sem((2 * ndp,)), sem((2 * ndp,)),

time: 37.7 us -> 38.6 us (1.024)
  Pallas kernels: 36.9 us -> 37.8 us
    pallas_call x1, Pallas kernels: 28.5 us -> 29.4 us  [on_device(): pl.pallas_call(functools.partial(inner, ndp, nten), out_shape=(jax.ShapeD...]
where the time goes in v5:
time: 38.6 us; the launch traced here: 38.4 us
  Pallas kernels  37.8 us (98%)
  between operations  0.64 us (2%)
    pallas_call x1, Pallas kernels, on_device(): pl.pallas_call(functools.partial(inner, ndp, nten), out_shape=(jax.ShapeD...  29.4 us
    pallas_call x1, Pallas kernels, on_device(): pl.pallas_call(functools.partial(closing, ndp), out_shape=(jax.ShapeDtype...  8.38 us

profile of v5, /device:TPU:0, one launch (start us, length us, event | category | flops | bytes accessed | tf_op | source)
XLA Modules:
  0.0 38.4 jit_solution(11492631640154308839)
XLA Ops:
  0.6 29.4 %shard_map.112 = (bf16[512,512]{1,0:T(8,128)(2,1)}, f32[8,2,8,128]{3,2,1,0:T(8,128)}) custom-call(bf16[512,4096]{1,0:T(8,128)(2,1)} %tok_hbm.1, bf16[512,1024]{1,0:T(8,128)(2,1)} %q_hbm.1, bf16[512,1024]{1,0:T(8,128)(2,1)} %o_hbm.1, bf16[4096,256]{1,0:T(8,128)(2,1)} %kw_hbm.3, bf16[4096,256]{1,0:T(8,128)(2,1)} %vw_hbm.3, f32[32,256]{1,0:T(8,128)} %ks_hbm.1, ...), custom_call_target="tpu_custom_call" | custom-call | tf_op jit(solution)/shard_map/pallas_call | solution.py:378
  30.0 8.4 %shard_map.113 = (bf16[512,4096]{1,0:T(8,128)(2,1)}, f32[32,64]{1,0:T(8,128)}, f32[32,64]{1,0:T(8,128)}) custom-call(bf16[512,512]{1,0:T(8,128)(2,1)} %get-tuple-element.5.low_hbm, bf16[4096,256]{1,0:T(8,128)(2,1)} %kw_hbm.3, bf16[4096,256]{1,0:T(8,128)(2,1)} %vw_hbm.3, f32[8,2,8,128]{3,2,1,0:T(8,128)} %get-tuple-element.6.sums), custom_call_target="tpu_custom_call" | custom-call | tf_op jit(solution)/shard_map/pallas_call | solution.py:417

commit v6 on v4

--- a/solution.py
+++ b/solution.py
@@ -18,7 +18,7 @@
 LONGEST = 256
 VMEM_LIMIT = 64 * 1024 * 1024
 TOGETHER = 4
-FB = 512
+FB = 1024
 KC = 4
 
 
@@ -69,13 +69,12 @@
         for i, (src, dst) in enumerate(((ks_hbm, ks), (vs_hbm, vs), (seg_hbm, seg), (tenants_hbm, tenants)))]
     for copy in small:
         copy.start()
+    load(tok_hbm, tok, pl.ds(0, half), slice(None), sem_t.at[0]).start()
     for k in range(KC):
         kk = pl.ds(k * kc, kc)
         load(kw_hbm, kw, kk, slice(None), sem_w.at[k]).start()
         load(vw_hbm, vw, kk, slice(None), sem_w.at[KC + k]).start()
-        load(tok_hbm, tok, pl.ds(0, half), kk, sem_t.at[k]).start()
-    for k in range(KC):
-        load(tok_hbm, tok, pl.ds(half, half), pl.ds(k * kc, kc), sem_t.at[KC + k]).start()
+    load(tok_hbm, tok, pl.ds(half, half), slice(None), sem_t.at[1]).start()
     for b in range(nb):
         loads["q", b].start()
         loads["o", b].start()
@@ -106,12 +105,14 @@
     def project(r, lo, hi):
         rr = pl.ds(r * half, half)
 
+        if lo == 0:
+            load(tok_hbm, tok, rr, slice(None), sem_t.at[r]).wait()
+
         def step(k, first):
             kk = pl.ds(pl.multiple_of(k * kc, kc), kc)
             if r == 0:
                 load(kw_hbm, kw, kk, slice(None), sem_w.at[k]).wait()
                 load(vw_hbm, vw, kk, slice(None), sem_w.at[KC + k]).wait()
-            load(tok_hbm, tok, rr, kk, sem_t.at[r * KC + k]).wait()
             block = tok[rr, kk]
             for kind, weight in ((0, kw), (1, vw)):
                 value = dot_nn(block, weight[kk, :])
@@ -338,8 +339,12 @@
     def load_value(i):
         return pltpu.make_async_copy(vw_hbm.at[at(i)], vw.at[at(i)], sem_v.at[i])
 
-    def save(i):
-        return pltpu.make_async_copy(grad.at[:, at(i)], grad_hbm.at[:, at(i)], sem_g.at[i])
+    half = grad.shape[0] // 2
+    group = min(2 * block, depth)
+
+    def save(r, g):
+        at_ = (pl.ds(r * half, half), pl.ds(g * group, group))
+        return pltpu.make_async_copy(grad.at[at_], grad_hbm.at[at_], sem_g.at[r * (depth // group) + g])
 
     load_low().start()
     for i in range(count):
@@ -347,15 +352,24 @@
         load_value(i).start()
     load_low().wait()
 
-    def step(i, _):
-        load_key(i).wait()
-        load_value(i).wait()
-        weights = jnp.concatenate([kw[at(i), :], vw[at(i), :]], axis=1)
-        grad[:, at(i)] = dot_nt(low[...], weights).astype(BF16)
-        save(i).start()
-        return 0
-
-    lax.fori_loop(0, count, step, 0)
+    wide = kw.shape[1]
+    saves = []
+    for r in range(2):
+        rr = pl.ds(r * half, half)
+
+        def step(i, _):
+            if r == 0:
+                load_key(i).wait()
+                load_value(i).wait()
+            value = dot_nt(low[rr, :wide], kw[at(i), :]) + dot_nt(low[rr, wide:], vw[at(i), :])
+            grad[rr, at(i)] = value.astype(BF16)
+            return 0
+
+        for g in range(depth // group):
+            each = group // block
+            lax.fori_loop(g * each, (g + 1) * each, step, 0)
+            saves.append(save(r, g))
+            saves[-1].start()
 
     tenant = lax.broadcasted_iota(jnp.int32, (NT, HD), 0).astype(F32)
     for kind, out in ((0, key_out), (1, value_out)):
@@ -365,8 +379,8 @@
             for s in range(SEQS):
                 total = total + jnp.where(tenant == rows[SEQS + s:SEQS + s + 1, :], rows[s:s + 1, :], 0.0)
         out[...] = total[:, :HD // 2]
-    for i in range(count):
-        save(i).wait()
+    for copy in saves:
+        copy.wait()
 
 
 def on_device(ndp, nten, tokens, queries, out_grad, key_weight, value_weight, key_scale, value_scale, segment_ids, tenant_ids):
@@ -407,7 +421,7 @@
             pltpu.VMEM(value_scale.shape, F32),
             pltpu.VMEM(segment_ids.shape, jnp.int32),
             pltpu.SMEM(tenant_ids.shape, jnp.int32),
-            sem((2 * KC,)), sem((2 * KC,)), sem((nb,)), sem((nb,)), sem((4,)), sem((2 * chips,)),
+            sem((2 * KC,)), sem((2,)), sem((nb,)), sem((nb,)), sem((4,)), sem((2 * chips,)),
             sem((nb,)), sem((nb,)), sem((many,)), sem((many,)), sem((nb,)), sem((nb,)), sem((nb,)), sem((nb,)),
             sem((nb,)), sem((nb,)), sem((many,)), sem((many,)), sem((many,)), sem((many,)),
             sem((2 * ndp,)), sem((2 * ndp,)),
@@ -431,7 +445,7 @@
             pltpu.VMEM(key_weight.shape, BF16),
             pltpu.VMEM(value_weight.shape, BF16),
             pltpu.VMEM((rows_all, depth), BF16),
-            sem((1,)), sem((count,)), sem((count,)), sem((count,)),
+            sem((1,)), sem((count,)), sem((count,)), sem((2 * count,)),
         ],
         compiler_params=pltpu.CompilerParams(vmem_limit_bytes=VMEM_LIMIT),
     )(low, key_weight, value_weight, sums)

time: 37.7 us -> 38.1 us (1.011)
  Pallas kernels: 36.9 us -> 37.3 us
    pallas_call x1, Pallas kernels: 28.5 us -> 28.9 us  [on_device(): pl.pallas_call(functools.partial(inner, ndp, nten), out_shape=(jax.ShapeD...]
where the time goes in v6:
time: 38.1 us; the launch traced here: 37.9 us
  Pallas kernels  37.3 us (98%)
  between operations  0.64 us (2%)
    pallas_call x1, Pallas kernels, on_device(): pl.pallas_call(functools.partial(inner, ndp, nten), out_shape=(jax.ShapeD...  28.9 us
    pallas_call x1, Pallas kernels, on_device(): pl.pallas_call(functools.partial(closing, ndp), out_shape=(jax.ShapeDtype...  8.33 us

profile of v6, /device:TPU:0, one launch (start us, length us, event | category | flops | bytes accessed | tf_op | source)
XLA Modules:
  0.0 37.9 jit_solution(892934737821516217)
XLA Ops:
  0.6 28.9 %shard_map.112 = (bf16[512,512]{1,0:T(8,128)(2,1)}, f32[8,2,8,128]{3,2,1,0:T(8,128)}) custom-call(bf16[512,4096]{1,0:T(8,128)(2,1)} %tok_hbm.1, bf16[512,1024]{1,0:T(8,128)(2,1)} %q_hbm.1, bf16[512,1024]{1,0:T(8,128)(2,1)} %o_hbm.1, bf16[4096,256]{1,0:T(8,128)(2,1)} %kw_hbm.3, bf16[4096,256]{1,0:T(8,128)(2,1)} %vw_hbm.3, f32[32,256]{1,0:T(8,128)} %ks_hbm.1, ...), custom_call_target="tpu_custom_call" | custom-call | tf_op jit(solution)/shard_map/pallas_call | solution.py:395
  29.6 8.3 %shard_map.113 = (bf16[512,4096]{1,0:T(8,128)(2,1)}, f32[32,64]{1,0:T(8,128)}, f32[32,64]{1,0:T(8,128)}) custom-call(bf16[512,512]{1,0:T(8,128)(2,1)} %get-tuple-element.5.low_hbm, bf16[4096,256]{1,0:T(8,128)(2,1)} %kw_hbm.3, bf16[4096,256]{1,0:T(8,128)(2,1)} %vw_hbm.3, f32[8,2,8,128]{3,2,1,0:T(8,128)} %get-tuple-element.6.sums), custom_call_target="tpu_custom_call" | custom-call | tf_op jit(solution)/shard_map/pallas_call | solution.py:434
